TPU v7x, 128 devices: a whole 4x4x4 slice. The times are simulated.
128 devices in a mesh: slab: 32 (over y, z, x_lo), run: 4 (over x_hi, core).
Axes of the slice: x: 4 (x_hi: 2, x_lo: 2; x = x_hi * 2 + x_lo), y: 4, z: 4, core: 2. Of those that a mesh axis runs over, the one named last changes fastest.
Arguments:
- material: int32 [128, 256, 256], P('slab'), may hold values from 0 to 15
- eps_table: float32 [16], replicated, may hold values from 1 to 12
- surface_mask: int32 [128], P('slab'), may hold values 0 or 1
- excite_map: int32 [4], P('run'), may hold values from 0 to 3
- mode_profiles: float32 [4, 256, 256], P(None, 'slab'), may hold values from -4 to 4
- port_eps: float32 [256, 256], P('slab'), may hold values from 1 to 4
- cotangent: float32 [4, 128, 256, 256], P('run', 'slab'), may hold values from -6 to 6
Outputs:
- gradient: float32 [128, 256, 256], P('slab')
- field_out: float32 [4, 128, 256, 256], P('run', 'slab')
Inputs may be any that keep to these rules, and one draw needn't show every extreme that they name: material indices into the permittivity table. `surface_mask`: 0 or 1 for each x layer. `excite_map`: an index of a mode profile.
All inputs are finite; a program needn't handle non-finite values. No bound on the sum of `surface_mask` on one device may be relied on, other than what follows from the above.
Results may differ from a plain program's by a relative error of at most 0.0001.
Values sent between devices are 32-bit elements; how exact they have to be, the bound alone decides.
A program may use at most 128 MiB of HBM per device.

v0:
```python
import jax
import jax.numpy as jnp
from jax import lax
from jax.sharding import PartitionSpec as P

STEPS = 6


time_step = 0.5


def padded_2(x, sides, width):
    for axis, dim in sides:
        size, length = (lax.axis_size(axis), x.shape[dim])
        up = [(i, (i + 1) % size) for i in range(size - 1)]
        down = [(j, i) for i, j in up]
        last = lax.slice_in_dim(x, length - width, length, axis=dim)
        first = lax.slice_in_dim(x, 0, width, axis=dim)
        before = lax.ppermute(last, axis, up)
        after = lax.ppermute(first, axis, down)
        x = jnp.concatenate([before, x, after], axis=dim)
    return x


def passed_along(block, axis, distance):
    devices = range(lax.axis_size(axis))
    route = [(i - distance, i) for i in devices if i - distance in devices]
    return lax.ppermute(block, axis, route)


def rim_zero(field, along):
    return jnp.zeros_like(lax.slice_in_dim(field, 0, 1, axis=along))


def ahead(field, along, border):
    length = field.shape[along]
    return jnp.concatenate([lax.slice_in_dim(field, 1, length, axis=along), border], along) - field


def behind(field, along, border):
    length = field.shape[along]
    return field - jnp.concatenate(
        [border, lax.slice_in_dim(field, 0, length - 1, axis=along)], along
    )


def update_magnetic(electric, magnetic, upper_y, upper_z):
    electric_x, electric_y, electric_z = electric
    magnetic_x, magnetic_y, magnetic_z = magnetic
    magnetic_x = magnetic_x - time_step * (
        ahead(electric_z, 2, rim_zero(electric_z, 2))
        - ahead(electric_y, 3, rim_zero(electric_y, 3))
    )
    magnetic_y = magnetic_y - time_step * (
        ahead(electric_x, 3, rim_zero(electric_x, 3)) - ahead(electric_z, 1, upper_z)
    )
    magnetic_z = magnetic_z - time_step * (
        ahead(electric_y, 1, upper_y) - ahead(electric_x, 2, rim_zero(electric_x, 2))
    )
    return (magnetic_x, magnetic_y, magnetic_z)


def update_electric(electric, magnetic, lower_y, lower_z, coefficient, source_y, source_z):
    electric_x, electric_y, electric_z = electric
    magnetic_x, magnetic_y, magnetic_z = magnetic
    electric_x = electric_x + coefficient * (
        behind(magnetic_z, 2, rim_zero(magnetic_z, 2))
        - behind(magnetic_y, 3, rim_zero(magnetic_y, 3))
    )
    electric_y = (
        electric_y
        + coefficient
        * (behind(magnetic_x, 3, rim_zero(magnetic_x, 3)) - behind(magnetic_z, 1, lower_z))
        + source_y
    )
    electric_z = (
        electric_z
        + coefficient
        * (behind(magnetic_y, 1, lower_y) - behind(magnetic_x, 2, rim_zero(magnetic_x, 2)))
        + source_z
    )
    return (electric_x, electric_y, electric_z)


def modal_advance(modal_now, modal_old, padded, port_coefficient, profile, forcing):
    middle = padded[1:-1]
    zpadded = jnp.pad(middle, ((0, 0), (1, 1)))
    laplacian = padded[2:] + padded[:-2] + zpadded[:, 2:] + zpadded[:, :-2] - 4.0 * middle
    return 2.0 * modal_now - modal_old + port_coefficient * laplacian + forcing * profile


def forcing_at(counter):
    moment = (counter + 1).astype(jnp.float32)
    return 2.0 * jnp.sin(0.3 * moment) * (1.0 - jnp.exp(-0.5 * moment))


def permittivity_of(material, eps_table):
    levels = jnp.arange(eps_table.shape[0], dtype=jnp.int32)
    picked = (material[None] == levels[:, None, None, None]).astype(jnp.float32)
    return jnp.sum(picked * eps_table[:, None, None, None], axis=0)


def local(material, eps_table, surface_mask, excite_map, mode_profiles, port_eps, cotangent):
    coefficient = time_step / permittivity_of(material, eps_table)
    mask_column = surface_mask.astype(jnp.float32)[:, None, None]
    injection = 0.25 * coefficient * mask_column
    selector = jnp.array([1.0, 0.0], jnp.float32)[:, None, None, None]
    choose = (jnp.arange(mode_profiles.shape[0], dtype=jnp.int32) == excite_map[0]).astype(
        jnp.float32
    )
    profile = jnp.sum(mode_profiles * choose[:, None, None], axis=0)
    port_coefficient = 0.25 / port_eps

    def port_step(modal_now, modal_old, forcing):
        padded = padded_2(modal_now, (("slab", 0),), 1)
        modal_next = modal_advance(modal_now, modal_old, padded, port_coefficient, profile, forcing)
        incident_e, incident_h = (
            lax.all_gather(modal_next, "slab", axis=0, tiled=True),
            lax.all_gather(modal_next - modal_now, "slab", axis=0, tiled=True),
        )
        return (modal_next, incident_e, incident_h)

    zeros = jnp.zeros((2,) + coefficient.shape, jnp.float32)
    electric = (zeros.at[0].set(cotangent[0]), zeros, zeros.at[1].set(cotangent[0]))
    magnetic = (zeros, zeros, zeros)
    modal_zero = jnp.zeros_like(profile)

    def advance(counter, carried):
        electric, magnetic, modal_now, modal_old, gradient_sum = carried
        modal_next, incident_e, incident_h = port_step(modal_now, modal_old, forcing_at(counter))
        electric_x, electric_y, electric_z = electric
        upper_rim = passed_along(
            jnp.concatenate([electric_y[:, 0:1], electric_z[:, 0:1]], 1), "slab", -1
        )
        magnetic = update_magnetic(electric, magnetic, upper_rim[:, 0:1], upper_rim[:, 1:2])
        lower_rim = passed_along(
            jnp.concatenate([magnetic[1][:, -1:], magnetic[2][:, -1:]], 1), "slab", 1
        )
        lower_y = lower_rim[:, 0:1]
        lower_z = lower_rim[:, 1:2]
        electric = update_electric(
            electric,
            magnetic,
            lower_y,
            lower_z,
            coefficient,
            selector * (injection * incident_h),
            selector * (injection * incident_e),
        )
        gradient_sum = gradient_sum + (
            electric[0][0] * electric[0][1]
            + electric[1][0] * electric[1][1]
            + electric[2][0] * electric[2][1]
        )
        return (electric, magnetic, modal_next, modal_now, gradient_sum)

    carried = lax.fori_loop(
        0,
        STEPS,
        advance,
        (electric, magnetic, modal_zero, modal_zero, jnp.zeros(coefficient.shape, jnp.float32)),
    )
    gradient = lax.psum(carried[4], "run")
    return (gradient, carried[0][1][0][None])


def solution(mesh):
    in_specs = (
        P("slab", None, None),
        P(),
        P("slab"),
        P("run"),
        P(None, "slab", None),
        P("slab", None),
        P("run", "slab", None, None),
    )
    out_specs = (P("slab", None, None), P("run", "slab", None, None))
    return jax.shard_map(local, mesh=mesh, in_specs=in_specs, out_specs=out_specs, check_vma=False)
```

profile of v0, /device:TPU:1, one launch (start us, length us, event | category | flops | bytes accessed | tf_op | source)
XLA Modules:
  0.0 1372.4 jit_solution(14720914317729965856)
XLA Ops:
  14.8 1125.8 %while.35 = (s32[]{:T(128)}, f32[2,4,256,256]{3,2,1,0:T(8,128)S(1)}, f32[2,4,256,256]{3,2,1,0:T(8,128)}, f32[2,4,256,256]{3,2,1,0:T(8,128)}, f32[2,4,256,256]{3,...) while((s32[]{:T(128)}, ...), condition=%wide.region_3.0_spmd.clone.clone, body=%wide.region_2.0_spmd.clone.clone.sunk | while | flops 25982984 | bytes 269106240 | solution.py:157
  20.4 23.2 %collective-permute-done = f32[2,2,256,256]{3,2,1,0:T(8,128)S(1)} collective-permute-done((f32[2,2,256,256]{3,2,1,0:T(8,128)S(1)}, f32[2,2,256,256]{3,2,1,0:T(8,128)S(1)}, u32[]{:S(2)}, u32[]{:S(2)}) %collective-permute-start) | collective-permute-done | bytes 1048608 | tf_op jit(solution)/shard_map/while/body/eval_jaxpr/ppermute | solution.py:28
  56.7 17.1 %collective-permute-done.2 = f32[1,256]{1,0:T(1,128)S(1)} collective-permute-done((f32[1,256]{1,0:T(1,128)S(1)}, f32[1,256]{1,0:T(1,128)S(1)}, u32[]{:S(2)}, u32[]{:S(2)}) %collective-permute-start.2) | collective-permute-done | bytes 1056 | tf_op jit(solution)/shard_map/while/body/eval_jaxpr/ppermute | solution.py:19
  75.6 69.1 %all_gather.26 = f32[256,256]{1,0:T(8,128)S(1)} all-gather(f32[8,256]{1,0:T(8,128)S(1)} %get-tuple-element.732), channel_id=1, replica_groups=mesh['slab'=32,'run'=4] {'slab'}, dimensions={0}, use_global_device_ids=true | all-gather | bytes 270336 | tf_op jit(solution)/shard_map/while/body/eval_jaxpr/all_gather | solution.py:118
  144.7 63.4 %all_gather.27 = f32[256,256]{1,0:T(8,128)S(1)} all-gather(f32[8,256]{1,0:T(8,128)S(1)} %get-tuple-element.676), channel_id=1, replica_groups=mesh['slab'=32,'run'=4] {'slab'}, dimensions={0}, use_global_device_ids=true | all-gather | bytes 270336 | tf_op jit(solution)/shard_map/while/body/eval_jaxpr/all_gather | solution.py:119
  226.3 12.8 collective-permute-done
  263.2 63.8 %all_gather.26 = f32[256,256]{1,0:T(8,128)S(1)} all-gather(f32[8,256]{1,0:T(8,128)S(1)} %get-tuple-element.732), channel_id=1, replica_groups=mesh['slab'=32,'run'=4] {'slab'}, dimensions={0}, use_global_device_ids=true | all-gather | bytes 270336 | tf_op jit(solution)/shard_map/while/body/eval_jaxpr/all_gather | solution.py:118
  327.0 65.1 %all_gather.27 = f32[256,256]{1,0:T(8,128)S(1)} all-gather(f32[8,256]{1,0:T(8,128)S(1)} %get-tuple-element.676), channel_id=1, replica_groups=mesh['slab'=32,'run'=4] {'slab'}, dimensions={0}, use_global_device_ids=true | all-gather | bytes 270336 | tf_op jit(solution)/shard_map/while/body/eval_jaxpr/all_gather | solution.py:119
  411.6 12.7 collective-permute-done
  435.3 8.9 collective-permute-done.2
  445.4 65.4 %all_gather.26 = f32[256,256]{1,0:T(8,128)S(1)} all-gather(f32[8,256]{1,0:T(8,128)S(1)} %get-tuple-element.732), channel_id=1, replica_groups=mesh['slab'=32,'run'=4] {'slab'}, dimensions={0}, use_global_device_ids=true | all-gather | bytes 270336 | tf_op jit(solution)/shard_map/while/body/eval_jaxpr/all_gather | solution.py:118
  510.8 63.5 %all_gather.27 = f32[256,256]{1,0:T(8,128)S(1)} all-gather(f32[8,256]{1,0:T(8,128)S(1)} %get-tuple-element.676), channel_id=1, replica_groups=mesh['slab'=32,'run'=4] {'slab'}, dimensions={0}, use_global_device_ids=true | all-gather | bytes 270336 | tf_op jit(solution)/shard_map/while/body/eval_jaxpr/all_gather | solution.py:119
  593.8 13.2 collective-permute-done
  619.5 8.9 collective-permute-done.2
  629.2 65.6 %all_gather.26 = f32[256,256]{1,0:T(8,128)S(1)} all-gather(f32[8,256]{1,0:T(8,128)S(1)} %get-tuple-element.732), channel_id=1, replica_groups=mesh['slab'=32,'run'=4] {'slab'}, dimensions={0}, use_global_device_ids=true | all-gather | bytes 270336 | tf_op jit(solution)/shard_map/while/body/eval_jaxpr/all_gather | solution.py:118
  694.9 64.3 %all_gather.27 = f32[256,256]{1,0:T(8,128)S(1)} all-gather(f32[8,256]{1,0:T(8,128)S(1)} %get-tuple-element.676), channel_id=1, replica_groups=mesh['slab'=32,'run'=4] {'slab'}, dimensions={0}, use_global_device_ids=true | all-gather | bytes 270336 | tf_op jit(solution)/shard_map/while/body/eval_jaxpr/all_gather | solution.py:119
  778.7 13.0 collective-permute-done
  813.4 65.3 %all_gather.26 = f32[256,256]{1,0:T(8,128)S(1)} all-gather(f32[8,256]{1,0:T(8,128)S(1)} %get-tuple-element.732), channel_id=1, replica_groups=mesh['slab'=32,'run'=4] {'slab'}, dimensions={0}, use_global_device_ids=true | all-gather | bytes 270336 | tf_op jit(solution)/shard_map/while/body/eval_jaxpr/all_gather | solution.py:118
  878.8 64.0 %all_gather.27 = f32[256,256]{1,0:T(8,128)S(1)} all-gather(f32[8,256]{1,0:T(8,128)S(1)} %get-tuple-element.676), channel_id=1, replica_groups=mesh['slab'=32,'run'=4] {'slab'}, dimensions={0}, use_global_device_ids=true | all-gather | bytes 270336 | tf_op jit(solution)/shard_map/while/body/eval_jaxpr/all_gather | solution.py:119
  962.3 12.9 collective-permute-done
  987.6 8.8 collective-permute-done.2
  997.6 65.0 %all_gather.26 = f32[256,256]{1,0:T(8,128)S(1)} all-gather(f32[8,256]{1,0:T(8,128)S(1)} %get-tuple-element.732), channel_id=1, replica_groups=mesh['slab'=32,'run'=4] {'slab'}, dimensions={0}, use_global_device_ids=true | all-gather | bytes 270336 | tf_op jit(solution)/shard_map/while/body/eval_jaxpr/all_gather | solution.py:118
  1062.7 63.9 %all_gather.27 = f32[256,256]{1,0:T(8,128)S(1)} all-gather(f32[8,256]{1,0:T(8,128)S(1)} %get-tuple-element.676), channel_id=1, replica_groups=mesh['slab'=32,'run'=4] {'slab'}, dimensions={0}, use_global_device_ids=true | all-gather | bytes 270336 | tf_op jit(solution)/shard_map/while/body/eval_jaxpr/all_gather | solution.py:119
  1142.9 220.3 %all-reduce.13.cloned.1.call-done = f32[4,256,256]{2,1,0:T(8,128)} async-done(((f32[4,256,256]{2,1,0:T(8,128)}), f32[4,256,256]{2,1,0:T(8,128)}) %all-reduce.13.cloned.1.call-update) | async-done | bytes 1048592 | tf_op jit(solution)/shard_map/psum | solution.py:163
  (476 shorter events, 224.2 us)
Async XLA Ops:
  7.2 1356.1 %all-reduce.13.cloned.1.call-start = ((), (), s32[]{:S(2)}) async-start(), calls=%async_computation | async-start | bytes 2097152 | tf_op jit(solution)/shard_map/psum | solution.py:163
  17.2 26.3 %collective-permute-start = (f32[2,2,256,256]{3,2,1,0:T(8,128)S(1)}, f32[2,2,256,256]{3,2,1,0:T(8,128)S(1)}, u32[]{:S(2)}, u32[]{:S(2)}) collective-permute-start(f32[2,2,256,256]{3,2,1,0:T(8,128)S(1)} %pad_maximum_fusion.6), channel_id=1, source_target_pairs={{4,0},{8,4},{12,8},{16,12},{20,16},{24,20},{28,24},{32,28},{36,32}... | collective-permute-start | bytes 3145736 | tf_op jit(solution)/shard_map/while/body/eval_jaxpr/ppermute | solution.py:28
  48.2 162.0 %collective-permute-start.1 = (f32[2,2,256,256]{3,2,1,0:T(8,128)}, f32[2,2,256,256]{3,2,1,0:T(8,128)}, u32[]{:S(2)}, u32[]{:S(2)}) collective-permute-start(f32[2,2,256,256]{3,2,1,0:T(8,128)} %pad_maximum_fusion.7), channel_id=1, source_target_pairs={{0,4},{4,8},{8,12},{12,16},{16,20},{20,24},{24,28},{28,32},{32,36}... | collective-permute-start | bytes 3145736 | tf_op jit(solution)/shard_map/while/body/eval_jaxpr/ppermute | solution.py:28
  53.6 20.2 %collective-permute-start.2 = (f32[1,256]{1,0:T(1,128)S(1)}, f32[1,256]{1,0:T(1,128)S(1)}, u32[]{:S(2)}, u32[]{:S(2)}) collective-permute-start(f32[1,256]{1,0:T(1,128)S(1)} %get-tuple-element.673), channel_id=1, source_target_pairs={{0,4},{4,8},{8,12},{12,16},{16,20},{20,24},{24,28},{28,32},{32,36}... | collective-permute-start | bytes 3080 | tf_op jit(solution)/shard_map/while/body/eval_jaxpr/ppermute | solution.py:19
  55.3 19.6 %collective-permute-start.3 = (f32[1,256]{1,0:T(1,128)S(1)}, f32[1,256]{1,0:T(1,128)S(1)}, u32[]{:S(2)}, u32[]{:S(2)}) collective-permute-start(f32[1,256]{1,0:T(1,128)S(1)} %get-tuple-element.674), channel_id=1, source_target_pairs={{4,0},{8,4},{12,8},{16,12},{20,16},{24,20},{28,24},{32,28},{36,32}... | collective-permute-start | bytes 3080 | tf_op jit(solution)/shard_map/while/body/eval_jaxpr/ppermute | solution.py:20
  223.1 16.0 %collective-permute-start = (f32[2,2,256,256]{3,2,1,0:T(8,128)S(1)}, f32[2,2,256,256]{3,2,1,0:T(8,128)S(1)}, u32[]{:S(2)}, u32[]{:S(2)}) collective-permute-start(f32[2,2,256,256]{3,2,1,0:T(8,128)S(1)} %pad_maximum_fusion.6), channel_id=1, source_target_pairs={{4,0},{8,4},{12,8},{16,12},{20,16},{24,20},{28,24},{32,28},{36,32}... | collective-permute-start | bytes 3145736 | tf_op jit(solution)/shard_map/while/body/eval_jaxpr/ppermute | solution.py:28
  243.7 150.5 %collective-permute-start.1 = (f32[2,2,256,256]{3,2,1,0:T(8,128)}, f32[2,2,256,256]{3,2,1,0:T(8,128)}, u32[]{:S(2)}, u32[]{:S(2)}) collective-permute-start(f32[2,2,256,256]{3,2,1,0:T(8,128)} %pad_maximum_fusion.7), channel_id=1, source_target_pairs={{0,4},{4,8},{8,12},{12,16},{16,20},{20,24},{24,28},{28,32},{32,36}... | collective-permute-start | bytes 3145736 | tf_op jit(solution)/shard_map/while/body/eval_jaxpr/ppermute | solution.py:28
  248.8 11.1 collective-permute-start.2
  250.1 12.5 collective-permute-start.3
  408.5 15.9 %collective-permute-start = (f32[2,2,256,256]{3,2,1,0:T(8,128)S(1)}, f32[2,2,256,256]{3,2,1,0:T(8,128)S(1)}, u32[]{:S(2)}, u32[]{:S(2)}) collective-permute-start(f32[2,2,256,256]{3,2,1,0:T(8,128)S(1)} %pad_maximum_fusion.6), channel_id=1, source_target_pairs={{4,0},{8,4},{12,8},{16,12},{20,16},{24,20},{28,24},{32,28},{36,32}... | collective-permute-start | bytes 3145736 | tf_op jit(solution)/shard_map/while/body/eval_jaxpr/ppermute | solution.py:28
  429.0 147.4 %collective-permute-start.1 = (f32[2,2,256,256]{3,2,1,0:T(8,128)}, f32[2,2,256,256]{3,2,1,0:T(8,128)}, u32[]{:S(2)}, u32[]{:S(2)}) collective-permute-start(f32[2,2,256,256]{3,2,1,0:T(8,128)} %pad_maximum_fusion.7), channel_id=1, source_target_pairs={{0,4},{4,8},{8,12},{12,16},{16,20},{20,24},{24,28},{28,32},{32,36}... | collective-permute-start | bytes 3145736 | tf_op jit(solution)/shard_map/while/body/eval_jaxpr/ppermute | solution.py:28
  432.6 11.6 collective-permute-start.2
  433.9 10.8 collective-permute-start.3
  590.6 16.4 %collective-permute-start = (f32[2,2,256,256]{3,2,1,0:T(8,128)S(1)}, f32[2,2,256,256]{3,2,1,0:T(8,128)S(1)}, u32[]{:S(2)}, u32[]{:S(2)}) collective-permute-start(f32[2,2,256,256]{3,2,1,0:T(8,128)S(1)} %pad_maximum_fusion.6), channel_id=1, source_target_pairs={{4,0},{8,4},{12,8},{16,12},{20,16},{24,20},{28,24},{32,28},{36,32}... | collective-permute-start | bytes 3145736 | tf_op jit(solution)/shard_map/while/body/eval_jaxpr/ppermute | solution.py:28
  611.6 149.6 %collective-permute-start.1 = (f32[2,2,256,256]{3,2,1,0:T(8,128)}, f32[2,2,256,256]{3,2,1,0:T(8,128)}, u32[]{:S(2)}, u32[]{:S(2)}) collective-permute-start(f32[2,2,256,256]{3,2,1,0:T(8,128)} %pad_maximum_fusion.7), channel_id=1, source_target_pairs={{0,4},{4,8},{8,12},{12,16},{16,20},{20,24},{24,28},{28,32},{32,36}... | collective-permute-start | bytes 3145736 | tf_op jit(solution)/shard_map/while/body/eval_jaxpr/ppermute | solution.py:28
  616.8 11.6 collective-permute-start.2
  618.1 10.5 collective-permute-start.3
  775.5 16.2 %collective-permute-start = (f32[2,2,256,256]{3,2,1,0:T(8,128)S(1)}, f32[2,2,256,256]{3,2,1,0:T(8,128)S(1)}, u32[]{:S(2)}, u32[]{:S(2)}) collective-permute-start(f32[2,2,256,256]{3,2,1,0:T(8,128)S(1)} %pad_maximum_fusion.6), channel_id=1, source_target_pairs={{4,0},{8,4},{12,8},{16,12},{20,16},{24,20},{28,24},{32,28},{36,32}... | collective-permute-start | bytes 3145736 | tf_op jit(solution)/shard_map/while/body/eval_jaxpr/ppermute | solution.py:28
  796.4 148.5 %collective-permute-start.1 = (f32[2,2,256,256]{3,2,1,0:T(8,128)}, f32[2,2,256,256]{3,2,1,0:T(8,128)}, u32[]{:S(2)}, u32[]{:S(2)}) collective-permute-start(f32[2,2,256,256]{3,2,1,0:T(8,128)} %pad_maximum_fusion.7), channel_id=1, source_target_pairs={{0,4},{4,8},{8,12},{12,16},{16,20},{20,24},{24,28},{28,32},{32,36}... | collective-permute-start | bytes 3145736 | tf_op jit(solution)/shard_map/while/body/eval_jaxpr/ppermute | solution.py:28
  801.0 11.4 collective-permute-start.2
  959.1 16.1 %collective-permute-start = (f32[2,2,256,256]{3,2,1,0:T(8,128)S(1)}, f32[2,2,256,256]{3,2,1,0:T(8,128)S(1)}, u32[]{:S(2)}, u32[]{:S(2)}) collective-permute-start(f32[2,2,256,256]{3,2,1,0:T(8,128)S(1)} %pad_maximum_fusion.6), channel_id=1, source_target_pairs={{4,0},{8,4},{12,8},{16,12},{20,16},{24,20},{28,24},{32,28},{36,32}... | collective-permute-start | bytes 3145736 | tf_op jit(solution)/shard_map/while/body/eval_jaxpr/ppermute | solution.py:28
  979.8 148.9 %collective-permute-start.1 = (f32[2,2,256,256]{3,2,1,0:T(8,128)}, f32[2,2,256,256]{3,2,1,0:T(8,128)}, u32[]{:S(2)}, u32[]{:S(2)}) collective-permute-start(f32[2,2,256,256]{3,2,1,0:T(8,128)} %pad_maximum_fusion.7), channel_id=1, source_target_pairs={{0,4},{4,8},{8,12},{12,16},{16,20},{20,24},{24,28},{28,32},{32,36}... | collective-permute-start | bytes 3145736 | tf_op jit(solution)/shard_map/while/body/eval_jaxpr/ppermute | solution.py:28
  984.9 11.6 collective-permute-start.2
  986.2 10.8 collective-permute-start.3
  (139 other events, 2057.4 us)
Sparse Core Ops, SparseCore 0:
  1140.7 222.4 all-reduce.12
where the time goes:
time: 1370 us
  blocking collectives  778 us (57%)
  waiting for transfers between devices  374 us (27%)
  other arithmetic  95.8 us (7%)
  local copies, waits for them, and re-layouts  53.6 us (4%)
  starting transfers between devices  52.5 us (4%)
  between operations  14.8 us (1%)
    all_gather x6, blocking collectives, port_step(): lax.all_gather(modal_next, 'slab', axis=0, tiled=True)  394 us
    all_gather x6, blocking collectives, port_step(): lax.all_gather(modal_next - modal_now, 'slab', axis=0, tiled=True)  384 us
    psum x1, waiting for transfers between devices, local(): gradient = lax.psum(carried[4], 'run')  220 us
    ppermute x12, waiting for transfers between devices, passed_along(): return lax.ppermute(block, axis, route)  87.8 us
    ppermute x6, waiting for transfers between devices, padded_2(): before = lax.ppermute(last, axis, up)  60.7 us
    ppermute x12, starting transfers between devices, passed_along(): return lax.ppermute(block, axis, route)  36.6 us
    add x6, other arithmetic, update_electric(): electric_z + coefficient * (behind(magnetic_y, 1, lower_y) - behind(magne...  31.7 us
  transfers between devices with their start and end apart: 25, of which 19 were waited for; matrix products, arithmetic and copies ran while one was open for 2% of the time, Pallas kernels for 0%

commit v1 on v0

v1 whole, which is shorter than its diff:
```python
import functools
import math

import jax
import jax.numpy as jnp
from jax import lax
from jax.experimental import pallas as pl
from jax.experimental.pallas import tpu as pltpu
from jax.sharding import PartitionSpec as P

STEPS = 6
F32 = jnp.float32
DEPTH = 4
LAYERS = 2 * DEPTH + 2 * STEPS
PAD = 8
FIRST = STEPS
LOOK = 4


def forcing_of(n):
    t = float(n + 1)
    return 2.0 * math.sin(0.3 * t) * (1.0 - math.exp(-0.5 * t))


def cuts(total, sizes):
    spans, at = [], 0
    for size in sizes:
        if at < total:
            spans.append((at, min(total, at + size)))
            at += size
    if at < total:
        spans.append((at, total))
    return spans


def kernel(
    slabs, grid_y, grid_z,
    eps_s, mask_s, excite_s, profiles_v, port_v, material_h, cot_h,
    grad_h, out_h,
    C, K, SK, MT, EX, EY, EZ, GX, GY, GZ, GR, W, gath, near, part, far, side, fin,
    load_sem, ag_send, ag_recv, xc_send, xc_recv, xk_send, xk_recv, z_send, z_recv,
    near_send, near_recv, far_send, far_recv, fin_copy, fin_send, fin_recv, fo_copy, fo_send, fo_recv,
):
    half = 4 * slabs
    tiles = slabs // 2 + 1
    rows_all = 8 * tiles
    pairs = slabs // 2
    in_chunks = cuts(tiles, (3, 3, 4, 4, 3))
    out_chunks = cuts(tiles - 1, (6, 5, 3, 2))
    s = lax.axis_index("slab")
    r = lax.axis_index("run")
    p = lax.rem(s, 2)
    m = s // 2
    core = lax.rem(r, 2)
    other_core = r + 1 - 2 * core
    other_run = lax.rem(r + 2, 4)
    mate = s + 1 - 2 * p
    py, pz = m // grid_z, lax.rem(m, grid_z)
    not_first, not_last = m > 0, m < pairs - 1
    window = p * (slabs // 2 - 1)
    base, mate_base = 8 * window, 8 * ((1 - p) * (slabs // 2 - 1))
    own, mates = FIRST + DEPTH * p, FIRST + DEPTH * (1 - p)

    def to(slab, run):
        return {"slab": slab, "run": run}

    def remote(src, dst, send, recv, slab, run):
        return pltpu.make_async_remote_copy(
            src_ref=src, dst_ref=dst, send_sem=send, recv_sem=recv,
            device_id=to(slab, run), device_id_type=pl.DeviceIdType.MESH,
        )

    def lanes(h):
        return pl.ds(128 * h, 128)

    def ds8(start, size):
        return pl.ds(pl.multiple_of(start, 8), size)

    loads = []
    for h in range(2):
        loads.append(pltpu.make_async_copy(material_h.at[:, :, lanes(h)], MT.at[:, h], load_sem.at[h]))
        loads.append(
            pltpu.make_async_copy(
                cot_h.at[0, :, ds8(base, rows_all), lanes(h)],
                C.at[pl.ds(own, DEPTH), h, pl.ds(PAD, rows_all), :],
                load_sem.at[2 + h],
            )
        )
    for copy in loads:
        copy.start()

    z_mates = [(py * grid_z + lax.rem(pz + d, grid_z)) * 2 + p for d in range(1, grid_z)]
    y_mates = [(lax.rem(py + d, grid_y) * grid_z + pz) * 2 + p for d in range(1, grid_y)]
    barrier = pltpu.get_barrier_semaphore()

    def hello(slab, run):
        pl.semaphore_signal(barrier, inc=1, device_id=to(slab, run), device_id_type=pl.DeviceIdType.MESH)

    hello(mate, r)
    hello(mate, other_run)
    hello(s, other_core)
    hello(s, other_run)
    for peer in z_mates + y_mates:
        hello(peer, r)

    @pl.when(not_first)
    def _():
        hello(s - 2, r)

    @pl.when(not_last)
    def _():
        hello(s + 2, r)

    picked = jnp.zeros((8, 256), F32)
    for j in range(4):
        picked = jnp.where(excite_s[0] == j, profiles_v[j], picked)
    port = 0.25 / port_v[...]
    for h in range(2):
        gath[s, h] = picked[:, 128 * h : 128 * h + 128]
        gath[s, 2 + h] = port[:, 128 * h : 128 * h + 128]

    zero_row = jnp.zeros((8, 128), F32)
    bottom = jnp.zeros((2, 2, 8, 128), F32)

    def clear(i, carry):
        C[i, :, pl.ds(PAD + rows_all, 8), :] = jnp.zeros((2, 8, 128), F32)
        return carry

    lax.fori_loop(0, LAYERS, clear, 0)

    def clear_fields(i, carry):
        EX[i, :, :, pl.ds(PAD + rows_all, 8), :] = bottom
        EZ[i, :, :, pl.ds(PAD + rows_all, 8), :] = bottom
        GX[i, :, :, pl.ds(0, 8), :] = bottom
        GZ[i, :, :, pl.ds(0, 8), :] = bottom
        return carry

    lax.fori_loop(0, LAYERS - 2, clear_fields, 0)
    GX[LAYERS - 2, :, :, pl.ds(0, 8), :] = bottom
    GZ[LAYERS - 2, :, :, pl.ds(0, 8), :] = bottom
    for n in range(STEPS):
        for edge in (0, PAD + rows_all):
            W[n, :, pl.ds(edge, 8), :] = jnp.zeros((2, 8, 128), F32)

    def clear_end(c_first, k_first):
        def one(t, carry):
            rows = ds8(8 * t, 8)
            C[pl.ds(c_first, STEPS), :, rows, :] = jnp.zeros((STEPS, 2, 8, 128), F32)
            K[pl.ds(k_first, STEPS - 1), :, rows, :] = jnp.zeros((STEPS - 1, 2, 8, 128), F32)
            return carry

        lax.fori_loop(0, tiles + 1, one, 0)

    @pl.when(m == 0)
    def _():
        clear_end(0, 0)

    @pl.when(m == pairs - 1)
    def _():
        clear_end(FIRST + 2 * DEPTH, FIRST + 2 * DEPTH - 1)

    def k_rows(c):
        start, stop = in_chunks[c]
        first = 0 if c == 0 else PAD + 8 * start
        return pl.ds(first, PAD + 8 * stop - first)

    def c_rows(c):
        start, stop = in_chunks[c]
        return pl.ds(PAD + 8 * start, 8 * (stop - start))

    for j in range(DEPTH):
        tile = jnp.full((8, 128), mask_s[j].astype(F32), F32)
        for h in range(2):
            SK[j, h, pl.ds(0, 8), :] = tile
            K[own - 1 + j, h, pl.ds(0, 8), :] = tile

    pl.semaphore_wait(
        barrier, 4 + (grid_z - 1) + (grid_y - 1) + not_first.astype(jnp.int32) + not_last.astype(jnp.int32)
    )

    ag_pair = remote(gath.at[s], gath.at[s], ag_send.at[0], ag_recv.at[0], mate, r)
    ag_pair.start()
    xc = []
    for c in range(len(in_chunks)):
        start, stop = in_chunks[c]
        for h in range(2):
            copy = remote(
                cot_h.at[0, :, ds8(mate_base + 8 * start, 8 * (stop - start)), lanes(h)],
                C.at[pl.ds(own, DEPTH), h, c_rows(c), :],
                xc_send.at[c, h], xc_recv.at[c, h], mate, r,
            )
            copy.start()
            xc.append(copy)

    table = [0.25 / jnp.full((1, 1, 8, 128), eps_s[j], F32) for j in range(16)]

    def coefficient_of(index):
        level = table
        for bit in range(4):
            odd = ((index >> bit) & 1) != 0
            level = [jnp.where(odd, level[2 * j + 1], level[2 * j]) for j in range(len(level) // 2)]
        return level[0]

    loads[0].wait()
    loads[2].wait()
    xk = []
    for c in range(len(in_chunks)):
        start, stop = in_chunks[c]

        def mates_rows(t, carry):
            SK[:, :, ds8(PAD + 8 * t, 8), :] = coefficient_of(MT[:, :, ds8(mate_base + 8 * t, 8), :])
            return carry

        lax.fori_loop(start, stop, mates_rows, 0)
        copy = remote(
            SK.at[:, :, k_rows(c), :], K.at[pl.ds(own - 1, DEPTH), :, k_rows(c), :],
            xk_send.at[c], xk_recv.at[c], mate, other_run,
        )
        copy.start()
        xk.append(copy)

    def own_rows(t, carry):
        K[pl.ds(own - 1, DEPTH), :, ds8(PAD + 8 * t, 8), :] = coefficient_of(MT[:, :, ds8(base + 8 * t, 8), :])
        return carry

    lax.fori_loop(0, tiles, own_rows, 0)

    remote(gath.at[mate], gath.at[mate], ag_send.at[0], ag_recv.at[0], mate, r).wait_recv()
    ag_z = []
    for d in range(1, grid_z):
        copy = remote(
            gath.at[pl.ds(2 * m, 2)], gath.at[pl.ds(2 * m, 2)], ag_send.at[d], ag_recv.at[d], z_mates[d - 1], r
        )
        copy.start()
        ag_z.append(copy)

    loads[1].wait()
    loads[3].wait()

    def z_copy(c, kind, up):
        if kind == 0:
            ref, rows, size = C, c_rows(c), STEPS
            src, dst = (FIRST + 2, 0) if up else (FIRST, FIRST + 2 * DEPTH)
        else:
            ref, rows, size = K, k_rows(c), STEPS - 1
            src, dst = (FIRST + 2, 0) if up else (FIRST - 1, FIRST + 2 * DEPTH - 1)
        way = 0 if up else 1
        return remote(
            ref.at[pl.ds(src, size), :, rows, :], ref.at[pl.ds(dst, size), :, rows, :],
            z_send.at[way, kind, c], z_recv.at[way, kind, c], s + 2 if up else s - 2, r,
        )

    def pass_on(c):
        start, stop = in_chunks[c]
        for h in range(2):
            remote(
                cot_h.at[0, :, ds8(mate_base + 8 * start, 8 * (stop - start)), lanes(h)],
                C.at[pl.ds(mates, DEPTH), h, c_rows(c), :],
                xc_send.at[c, h], xc_recv.at[c, h], mate, r,
            ).wait_recv()
        remote(
            SK.at[:, :, k_rows(c), :], K.at[pl.ds(mates - 1, DEPTH), :, k_rows(c), :],
            xk_send.at[c], xk_recv.at[c], mate, other_run,
        ).wait_recv()

        @pl.when(not_last)
        def _():
            for kind in range(2):
                z_copy(c, kind, True).start()

        @pl.when(not_first)
        def _():
            for kind in range(2):
                z_copy(c, kind, False).start()

    def halo_wait(c):
        @pl.when(not_first)
        def _():
            for kind in range(2):
                z_copy(c, kind, True).wait_recv()

        @pl.when(not_last)
        def _():
            for kind in range(2):
                z_copy(c, kind, False).wait_recv()

    pass_on(0)

    for d in range(1, grid_z):
        source = (py * grid_z + lax.rem(pz - d + grid_z, grid_z)) * 2
        remote(
            gath.at[pl.ds(source, 2)], gath.at[pl.ds(source, 2)], ag_send.at[d], ag_recv.at[d], z_mates[d - 1], r
        ).wait_recv()

    group = 2 * grid_z

    def whole(y):
        return jnp.where(p == 0, y < grid_y // 2, y >= grid_y // 2)

    def single(y):
        return y == grid_y // 2 - p

    single_slot = slabs // 2 - p

    def y_copy(d, y, full):
        slots = pl.ds(group * y, group) if full else pl.ds(single_slot, 1)
        return remote(
            gath.at[slots], gath.at[slots], ag_send.at[grid_z + d - 1], ag_recv.at[grid_z + d - 1], y_mates[d - 1], r
        )

    def y_each(y, action):
        @pl.when(whole(y))
        def _():
            action(True)

        @pl.when(single(y))
        def _():
            action(False)

    for d in range(1, grid_y):
        y_each(py, lambda full: y_copy(d, py, full).start())
    for c in range(1, len(in_chunks)):
        if in_chunks[c][0] - 1 - LOOK < 0:
            pass_on(c)
    for d in range(1, grid_y):
        source = lax.rem(py - d + grid_y, grid_y)
        y_each(source, lambda full: y_copy(d, source, full).wait_recv())

    lane = lax.broadcasted_iota(jnp.int32, (1, 1, 8, 128), 3)
    is_last, is_first = lane == 127, lane == 0

    def up_z(v):
        turned = pltpu.roll(v, 127, v.ndim - 1)
        follow = jnp.concatenate([turned[1:2], jnp.zeros_like(turned[1:2])], 0)
        return jnp.where(is_last if v.ndim == 4 else is_last[0], follow, turned)

    def down_z(v):
        turned = pltpu.roll(v, 1, v.ndim - 1)
        before = jnp.concatenate([jnp.zeros_like(turned[0:1]), turned[0:1]], 0)
        return jnp.where(is_first if v.ndim == 4 else is_first[0], before, turned)

    for n in range(STEPS):

        def port_rows(t, carry):
            rows = ds8(PAD + 8 * t, 8)
            slot = window + t
            drive = (0.5 * forcing_of(n)) * gath[slot, pl.ds(0, 2)]
            if n == 0:
                W[0, :, rows, :] = drive
                return carry
            now = W[n - 1, :, rows, :]
            after = W[n - 1, :, pl.ds(PAD + 8 * t + 1, 8), :]
            before = W[n - 1, :, pl.ds(PAD + 8 * t - 1, 8), :]
            laplacian = after + before + up_z(now) + down_z(now) - 4.0 * now
            value = 2.0 * now + gath[slot, pl.ds(2, 2)] * laplacian + drive
            if n > 1:
                value = value - W[n - 2, :, rows, :]
            W[n, :, rows, :] = value
            return carry

        lax.fori_loop(0, tiles, port_rows, 0)

    inside = not_first.astype(F32)

    def source_of(n, rows):
        ie = W[n - 1, :, rows, :]
        ih = ie if n == 1 else ie - W[n - 2, :, rows, :]
        return ie, ih

    def add_driven(v, extra):
        return jnp.concatenate([v[:, 0:1] + extra[:, None], v[:, 1:2]], 1)

    def product(a):
        return a[:, 0] * a[:, 1]

    def first_step(t):
        rows = ds8(PAD + 8 * t, 8)
        ahead_rows, behind_rows = pl.ds(PAD + 8 * t + 1, 8), pl.ds(PAD + 8 * t - 1, 8)
        ie, ih = source_of(1, rows)
        zero = jnp.zeros((2, 8, 128), F32)
        both = lambda d, e: jnp.stack([d, e], 1)
        follow = C[0, :, rows, :]
        gx_l = gy_l = gyd_l = None
        for i in range(LAYERS - 1):
            c = follow
            follow = C[i + 1, :, rows, :]
            gx = c - C[i, :, ahead_rows, :]
            gy = follow - c
            gyd = c - up_z(c)
            GX[i, :, :, rows, :] = both(zero, gx)
            GY[i, :, :, rows, :] = both(gyd, gy)
            GZ[i, :, :, rows, :] = both(-gx, zero)
            if i >= 1:
                if i == FIRST:
                    gx_l, gy_l, gyd_l = gx_l * inside, gy_l * inside, gyd_l * inside
                k = K[i - 1, :, rows, :]
                mask = K[i - 1, 0:1, pl.ds(0, 8), :]
                gx_y = gx - GX[i, :, 1, behind_rows, :]
                ex_d = c - k * (gx_y + (gyd - down_z(gyd)))
                ey_d = k * ((gx - gx_l) + mask * ih)
                ez_d = k * ((gyd - gyd_l) + mask * ie)
                ex_s = k * (down_z(gy) - gy)
                ey_s = k * (gx - down_z(gx))
                ez_s = c + k * ((gy - gy_l) - gx_y)
                EX[i - 1, :, :, rows, :] = both(ex_d, ex_s)
                EY[i - 1, :, :, rows, :] = both(ey_d, ey_s)
                EZ[i - 1, :, :, rows, :] = both(ez_d, ez_s)
                if FIRST <= i < FIRST + 2 * DEPTH:
                    GR[i - FIRST, :, rows, :] = ex_d * ex_s + ey_d * ey_s + ez_d * ez_s
            gx_l, gy_l, gyd_l = gx, gy, gyd

    def later_step(n, t):
        rows = ds8(PAD + 8 * t, 8)
        ahead_rows, behind_rows = pl.ds(PAD + 8 * t + 1, 8), pl.ds(PAD + 8 * t - 1, 8)
        ie, ih = source_of(n, rows)
        ey_n, ez_n = EY[n - 2, :, :, rows, :], EZ[n - 2, :, :, rows, :]
        gy_l = gz_l = None
        for i in range(n - 1, LAYERS - n):
            ex, ey, ez = EX[i - 1, :, :, rows, :], ey_n, ez_n
            ey_n, ez_n = EY[i, :, :, rows, :], EZ[i, :, :, rows, :]
            gx = GX[i, :, :, rows, :] + ((ez - EZ[i - 1, :, :, ahead_rows, :]) + (up_z(ey) - ey))
            gy = GY[i, :, :, rows, :] + ((ex - up_z(ex)) + (ez_n - ez))
            gz = GZ[i, :, :, rows, :] + ((ey - ey_n) + (EX[i - 1, :, :, ahead_rows, :] - ex))
            GX[i, :, :, rows, :] = gx
            GY[i, :, :, rows, :] = gy
            GZ[i, :, :, rows, :] = gz
            if i >= n:
                if i == FIRST:
                    gy_l, gz_l = gy_l * inside, gz_l * inside
                k = K[i - 1, :, rows, :][:, None]
                mask = K[i - 1, 0:1, pl.ds(0, 8), :]
                ex = ex + k * ((gz - GZ[i, :, :, behind_rows, :]) - (gy - down_z(gy)))
                ey = ey + k * add_driven((gx - down_z(gx)) - (gz - gz_l), mask * ih)
                ez = ez + k * add_driven((gy - gy_l) - (gx - GX[i, :, :, behind_rows, :]), mask * ie)
                EX[i - 1, :, :, rows, :] = ex
                EY[i - 1, :, :, rows, :] = ey
                EZ[i - 1, :, :, rows, :] = ez
                if FIRST <= i < FIRST + 2 * DEPTH:
                    GR[i - FIRST, :, rows, :] = GR[i - FIRST, :, rows, :] + (product(ex) + product(ey) + product(ez))
            gy_l, gz_l = gy, gz

    def near_copy(j):
        first, stop = out_chunks[j]
        return remote(
            GR.at[:, 1 - core, ds8(PAD + 8 * (p + first), 8 * (stop - first)), :],
            near.at[:, pl.ds(8 * first, 8 * (stop - first)), :],
            near_send.at[j], near_recv.at[j], s, other_core,
        )

    def far_copies(j):
        first, stop = out_chunks[j]
        rows = pl.ds(8 * first, 8 * (stop - first))
        mine, theirs = pl.ds(DEPTH * p, DEPTH), pl.ds(DEPTH * (1 - p), DEPTH)
        return [
            remote(part.at[mine, rows, :], far.at[:, rows, :], far_send.at[0, j], far_recv.at[0, j], s, other_run),
            remote(part.at[theirs, rows, :], side.at[0, :, rows, :], far_send.at[1, j], far_recv.at[1, j], mate, r),
            remote(
                part.at[theirs, rows, :], side.at[1, :, rows, :], far_send.at[2, j], far_recv.at[2, j], mate, other_run
            ),
        ]

    def fin_copies(j):
        first, stop = out_chunks[j]
        copies = []
        for k in range(2):
            rows = ds8(half * k + 8 * first, 8 * (stop - first))
            src = fin.at[:, rows, :]
            dst = grad_h.at[:, rows, pl.ds(pl.multiple_of(128 * core, 128), 128)]
            copies.append(
                (
                    pltpu.make_async_copy(src, dst, fin_copy.at[k, j]),
                    remote(src, dst, fin_send.at[k, j], fin_recv.at[k, j], s, other_core),
                    remote(
                        src, grad_h.at[:, rows, pl.ds(pl.multiple_of(128 * (1 - core), 128), 128)],
                        fin_send.at[k, j], fin_recv.at[k, j], s, other_core,
                    ),
                )
            )
        return copies

    def field_copies(j):
        first, stop = out_chunks[j]
        size = 8 * (stop - first)
        copies = []
        for h in range(2):
            src_rows = ds8(PAD + 8 * (p + first), size)
            dst = out_h.at[0, :, ds8(half * p + 8 * first, size), lanes(h)]
            back = out_h.at[0, :, ds8(half * (1 - p) + 8 * first, size), lanes(h)]
            src = EY.at[pl.ds(mates - 1, DEPTH), h, 0, src_rows, :]
            copies.append(
                (
                    pltpu.make_async_copy(EY.at[pl.ds(own - 1, DEPTH), h, 0, src_rows, :], dst, fo_copy.at[h, j]),
                    remote(src, dst, fo_send.at[h, j], fo_recv.at[h, j], mate, r),
                    remote(src, back, fo_send.at[h, j], fo_recv.at[h, j], mate, r),
                )
            )
        return copies

    def rows_done(j):
        near_copy(j).start()
        for here, there, _ in field_copies(j):
            there.start()
            here.start()

    def sum_cores(j):
        first, stop = out_chunks[j]
        near_copy(j).wait_recv()

        def one(t, carry):
            rows = ds8(8 * t, 8)
            part[:, rows, :] = GR[:, core, ds8(PAD + 8 * (p + t), 8), :] + near[:, rows, :]
            return carry

        lax.fori_loop(first, stop, one, 0)
        for copy in far_copies(j):
            copy.start()

    def sum_chips(j):
        first, stop = out_chunks[j]
        for copy in far_copies(j):
            copy.wait_recv()

        def one(t, carry):
            rows = ds8(8 * t, 8)
            fin[:, ds8(half * p + 8 * t, 8), :] = part[pl.ds(DEPTH * p, DEPTH), rows, :] + far[:, rows, :]
            fin[:, ds8(half * (1 - p) + 8 * t, 8), :] = side[0, :, rows, :] + side[1, :, rows, :]
            return carry

        lax.fori_loop(first, stop, one, 0)
        for here, there, _ in fin_copies(j):
            there.start()
            here.start()

    sweeps = tiles + STEPS - 1
    before, after, late = {}, {}, []
    for c in range(1, len(in_chunks)):
        at = in_chunks[c][0] - 1
        if at - LOOK >= 0:
            before.setdefault(at - LOOK, []).append(functools.partial(pass_on, c))
        before.setdefault(at, []).append(functools.partial(halo_wait, c))
    for j in range(len(out_chunks)):
        at = out_chunks[j][1] + STEPS - 1
        for event, delay in ((rows_done, 0), (sum_cores, 2), (sum_chips, 5)):
            if at + delay < sweeps:
                after.setdefault(at + delay, []).append(functools.partial(event, j))
            else:
                late.append((at + delay, functools.partial(event, j)))
    late.sort(key=lambda item: item[0])

    def at_sweep(T, table_of):
        for at, events in sorted(table_of.items()):

            @pl.when(T == at)
            def _():
                for event in events:
                    event()

    halo_wait(0)

    def sweep(T, carry):
        at_sweep(T, before)
        for n in range(1, STEPS + 1):
            t = T - (n - 1)
            high = tiles - 2 + p if n == STEPS else tiles - 1

            @pl.when((t >= 0) & (t <= high))
            def _():
                first_step(t) if n == 1 else later_step(n, t)

        at_sweep(T, after)
        return carry

    lax.fori_loop(0, sweeps, sweep, 0)
    for _, event in late:
        event()

    for j in range(len(out_chunks)):
        for here, there, back in fin_copies(j) + field_copies(j):
            here.wait()
            there.wait_send()
            back.wait_recv()
        near_copy(j).wait_send()
        for copy in far_copies(j):
            copy.wait_send()
    for copy in xc + xk + ag_z + [ag_pair]:
        copy.wait_send()
    for d in range(1, grid_y):
        y_each(py, lambda full: y_copy(d, py, full).wait_send())
    for c in range(len(in_chunks)):

        @pl.when(not_last)
        def _():
            for kind in range(2):
                z_copy(c, kind, True).wait_send()

        @pl.when(not_first)
        def _():
            for kind in range(2):
                z_copy(c, kind, False).wait_send()


def local(slabs, grid_y, grid_z, material, eps_table, surface_mask, excite_map, mode_profiles, port_eps, cotangent):
    tiles = slabs // 2 + 1
    height = 8 * tiles + 2 * PAD
    half, rows = 4 * slabs, 8 * slabs
    chunks, outs = len(cuts(tiles, (3, 3, 4, 4, 3))), len(cuts(tiles - 1, (6, 5, 3, 2)))
    vmem = lambda *shape: pltpu.VMEM(shape, F32)
    dma = lambda *shape: pltpu.SemaphoreType.DMA(shape)
    field = lambda layers: vmem(layers, 2, 2, height, 128)
    smem_spec = pl.BlockSpec(memory_space=pltpu.SMEM)
    vmem_spec = pl.BlockSpec(memory_space=pltpu.VMEM)
    any_spec = pl.BlockSpec(memory_space=pl.ANY)
    scratch = [
        vmem(LAYERS, 2, height, 128),
        vmem(LAYERS - 2, 2, height, 128),
        vmem(DEPTH, 2, height, 128),
        pltpu.VMEM((DEPTH, 2, rows, 128), jnp.int32),
        field(LAYERS - 2), field(LAYERS - 2), field(LAYERS - 2),
        field(LAYERS - 1), field(LAYERS - 1), field(LAYERS - 1),
        vmem(2 * DEPTH, 2, height, 128),
        vmem(STEPS, 2, height, 128),
        vmem(slabs, 4, 8, 128),
        vmem(2 * DEPTH, half, 128), vmem(2 * DEPTH, half, 128),
        vmem(DEPTH, half, 128), vmem(2, DEPTH, half, 128), vmem(DEPTH, rows, 128),
        dma(4), dma(grid_z + grid_y - 1), dma(grid_z + grid_y - 1),
        dma(chunks, 2), dma(chunks, 2), dma(chunks), dma(chunks), dma(2, 2, chunks), dma(2, 2, chunks),
        dma(outs), dma(outs), dma(3, outs), dma(3, outs),
        dma(2, outs), dma(2, outs), dma(2, outs), dma(2, outs), dma(2, outs), dma(2, outs),
    ]
    return pl.pallas_call(
        functools.partial(kernel, slabs, grid_y, grid_z),
        out_shape=(
            jax.ShapeDtypeStruct(material.shape, F32),
            jax.ShapeDtypeStruct(cotangent.shape, F32),
        ),
        in_specs=[smem_spec, smem_spec, smem_spec, vmem_spec, vmem_spec, any_spec, any_spec],
        out_specs=(any_spec, any_spec),
        scratch_shapes=scratch,
        compiler_params=pltpu.CompilerParams(
            collective_id=0, has_side_effects=True, vmem_limit_bytes=60 * 1024 * 1024
        ),
        cost_estimate=pl.CostEstimate(flops=600_000_000, bytes_accessed=6_000_000, transcendentals=0),
    )(eps_table, surface_mask, excite_map, mode_profiles, port_eps, material, cotangent)


def solution(mesh):
    slabs = mesh.shape["slab"]
    grid_z = 4 if slabs == 32 else 2
    grid_y = slabs // 2 // grid_z
    in_specs = (
        P("slab", None, None),
        P(),
        P("slab"),
        P("run"),
        P(None, "slab", None),
        P("slab", None),
        P("run", "slab", None, None),
    )
    out_specs = (P("slab", None, None), P("run", "slab", None, None))
    return jax.shard_map(
        functools.partial(local, slabs, grid_y, grid_z),
        mesh=mesh, in_specs=in_specs, out_specs=out_specs, check_vma=False,
    )
```

time: 1370 us -> 115 us (0.08)
  blocking collectives: 778 us -> 0 us
  waiting for transfers between devices: 374 us -> 0 us
  Pallas kernels: 0 us -> 110 us
  other arithmetic: 95.8 us -> 0 us
  starting transfers between devices: 52.5 us -> 0 us
  local copies, waits for them, and re-layouts: 53.6 us -> 3.35 us
    all_gather x12 -> x0, blocking collectives: 778 us -> none  [the longest x6 394 us: port_step(): lax.all_gather(modal_next, 'slab', axis=0, tiled=True)]
    psum x1 -> x0, waiting for transfers between devices: 220 us -> none  [local(): gradient = lax.psum(carried[4], 'run')]
    ppermute x24 -> x0, waiting for transfers between devices: 154 us -> none  [the longest x12 87.8 us: passed_along(): return lax.ppermute(block, axis, route)]
    pallas_call x0 -> x1, Pallas kernels: none -> 110 us  [local(): pl.pallas_call(functools.partial(kernel, slabs, grid_y, grid_z), out_shap...]
    ppermute x24 -> x0, starting transfers between devices: 52.4 us -> none  [the longest x12 36.6 us: passed_along(): return lax.ppermute(block, axis, route)]
    add x12 -> x0, other arithmetic: 51.6 us -> none  [the longest x6 31.7 us: update_electric(): electric_z + coefficient * (behind(magnetic_y, 1, lower_y) - behind(magne...]
    slice x97 -> x0, local copies, waits for them, and re-layouts: 31.9 us -> none  [the longest x6 15.5 us: advance(): lower_y = lower_rim[:, 0:1]]
    while x258 -> x0, local copies, waits for them, and re-layouts: 16 us -> none
  transfers between devices with their start and end apart: 25 -> 0, of which waited for: 19 -> 0; matrix products, arithmetic and copies ran while one was open for 2% -> 0% of each run, Pallas kernels for 0% -> 0%
where the time goes in v1:
time: 115 us
  Pallas kernels  110 us (96%)
  local copies, waits for them, and re-layouts  3.35 us (3%)
  between operations  1.29 us (1%)
    pallas_call x1, Pallas kernels, local(): pl.pallas_call(functools.partial(kernel, slabs, grid_y, grid_z), out_shap...  110 us
    unnamed x4, local copies, waits for them, and re-layouts  3.35 us

profile of v1, /device:TPU:1, one launch (start us, length us, event | category | flops | bytes accessed | tf_op | source)
XLA Modules:
  0.0 114.7 jit_solution(9545811215737270)
XLA Ops:
  1.3 110.0 %shard_map.86 = (f32[4,256,256]{2,1,0:T(8,128)}, f32[1,4,256,256]{3,2,1,0:T(8,128)}) custom-call(f32[16]{0:T(128)} %eps_s.1, s32[4]{0:T(128)} %mask_s.1, s32[1]{0:T(128)S(6)} %copy.11.excite_s, f32[4,8,256]{2,1,0:T(8,128)} %profiles_v.1, f32[8,256]{1,0:T(8,128)} %port_v.1, s32[4,256,256]{2,1,0:T(8,128)} %material_h.1, f32[1,4,256,256]{3,2,1,0:T(8,128)} %cot_h.1), custom_call_target="tpu_custom_call" | custom-call | flops 600000000 | bytes 6000000 | tf_op jit(solution)/shard_map/pallas_call | solution.py:630
  111.3 0.0 copy-start
  111.3 2.4 %copy.12 = f32[4,256,256]{2,1,0:T(8,128)} copy(f32[4,256,256]{2,1,0:T(8,128)} %get-tuple-element.4) | data formatting | bytes 2097152
  113.7 0.0 copy-done
  113.7 1.0 copy.13
Async XLA Ops:
  111.3 2.4 %copy-start = (f32[1,4,256,256]{3,2,1,0:T(8,128)S(1)}, f32[1,4,256,256]{3,2,1,0:T(8,128)}, u32[]{:S(2)}) copy-start(f32[1,4,256,256]{3,2,1,0:T(8,128)} %get-tuple-element.5) | copy-start | bytes 3145732

commit v2 on v1

--- a/solution.py
+++ b/solution.py
@@ -14,7 +14,9 @@
 LAYERS = 2 * DEPTH + 2 * STEPS
 PAD = 8
 FIRST = STEPS
-LOOK = 4
+IN_SIZES = (2, 3, 4, 4, 4)
+OUT_SIZES = (4, 4, 4, 2, 2)
+PASS_AT = (-1, -1, 0, 2, 5)
 
 
 def forcing_of(n):
@@ -33,20 +35,41 @@
     return spans
 
 
+def z_order(back):
+    z = lax.broadcasted_iota(jnp.int32, (256, 256), 1 if back else 0)
+    place = lax.broadcasted_iota(jnp.int32, (256, 256), 0 if back else 1)
+    return (z == 2 * (place % 128) + place // 128).astype(F32).astype(jnp.bfloat16)
+
+
+def reorder(v, order):
+    high = v.astype(jnp.bfloat16)
+    rest = v - high.astype(F32)
+    middle = rest.astype(jnp.bfloat16)
+    low = (rest - middle.astype(F32)).astype(jnp.bfloat16)
+    dot = lambda part: jnp.dot(part, order, preferred_element_type=F32)
+    return (dot(high) + dot(middle)) + dot(low)
+
+
+def restore(grad_p, field_p, grad, field):
+    order = z_order(True)
+    grad[0] = reorder(jnp.concatenate([grad_p[0, 0], grad_p[0, 1]], 1), order)
+    field[0, 0] = reorder(jnp.concatenate([field_p[0, 0], field_p[0, 1]], 1), order)
+
+
 def kernel(
     slabs, grid_y, grid_z,
     eps_s, mask_s, excite_s, profiles_v, port_v, material_h, cot_h,
     grad_h, out_h,
-    C, K, SK, MT, EX, EY, EZ, GX, GY, GZ, GR, W, gath, near, part, far, side, fin,
-    load_sem, ag_send, ag_recv, xc_send, xc_recv, xk_send, xk_recv, z_send, z_recv,
+    C, K, SC, SK, MT, CR, EX, EY, EZ, GX, GY, GZ, GR, W, gath, near, part, far, side, fin,
+    load_sem, ag_send, ag_recv, xc_send, xc_recv, xk_send, xk_recv, z_send, z_recv, sib_send, sib_recv,
     near_send, near_recv, far_send, far_recv, fin_copy, fin_send, fin_recv, fo_copy, fo_send, fo_recv,
 ):
     half = 4 * slabs
     tiles = slabs // 2 + 1
     rows_all = 8 * tiles
     pairs = slabs // 2
-    in_chunks = cuts(tiles, (3, 3, 4, 4, 3))
-    out_chunks = cuts(tiles - 1, (6, 5, 3, 2))
+    in_chunks = cuts(tiles, IN_SIZES)
+    out_chunks = cuts(tiles - 1, OUT_SIZES)
     s = lax.axis_index("slab")
     r = lax.axis_index("run")
     p = lax.rem(s, 2)
@@ -70,24 +93,13 @@
             device_id=to(slab, run), device_id_type=pl.DeviceIdType.MESH,
         )
 
-    def lanes(h):
-        return pl.ds(128 * h, 128)
-
     def ds8(start, size):
         return pl.ds(pl.multiple_of(start, 8), size)
 
-    loads = []
-    for h in range(2):
-        loads.append(pltpu.make_async_copy(material_h.at[:, :, lanes(h)], MT.at[:, h], load_sem.at[h]))
-        loads.append(
-            pltpu.make_async_copy(
-                cot_h.at[0, :, ds8(base, rows_all), lanes(h)],
-                C.at[pl.ds(own, DEPTH), h, pl.ds(PAD, rows_all), :],
-                load_sem.at[2 + h],
-            )
-        )
-    for copy in loads:
-        copy.start()
+    load_cot = pltpu.make_async_copy(cot_h.at[0], CR, load_sem.at[0])
+    load_material = pltpu.make_async_copy(material_h, MT, load_sem.at[1])
+    load_cot.start()
+    load_material.start()
 
     z_mates = [(py * grid_z + lax.rem(pz + d, grid_z)) * 2 + p for d in range(1, grid_z)]
     y_mates = [(lax.rem(py + d, grid_y) * grid_z + pz) * 2 + p for d in range(1, grid_y)]
@@ -115,9 +127,11 @@
     for j in range(4):
         picked = jnp.where(excite_s[0] == j, profiles_v[j], picked)
     port = 0.25 / port_v[...]
+    order = z_order(False)
+    port_block = reorder(jnp.concatenate([picked, port], 0), order)
     for h in range(2):
-        gath[s, h] = picked[:, 128 * h : 128 * h + 128]
-        gath[s, 2 + h] = port[:, 128 * h : 128 * h + 128]
+        gath[s, h] = port_block[0:8, 128 * h : 128 * h + 128]
+        gath[s, 2 + h] = port_block[8:16, 128 * h : 128 * h + 128]
 
     zero_row = jnp.zeros((8, 128), F32)
     bottom = jnp.zeros((2, 2, 8, 128), F32)
@@ -170,8 +184,8 @@
 
     for j in range(DEPTH):
         tile = jnp.full((8, 128), mask_s[j].astype(F32), F32)
+        SK[j, pl.ds(0, 8), :] = tile
         for h in range(2):
-            SK[j, h, pl.ds(0, 8), :] = tile
             K[own - 1 + j, h, pl.ds(0, 8), :] = tile
 
     pl.semaphore_wait(
@@ -180,50 +194,59 @@
 
     ag_pair = remote(gath.at[s], gath.at[s], ag_send.at[0], ag_recv.at[0], mate, r)
     ag_pair.start()
+
+    def cot_rows(c, first):
+        start, stop = in_chunks[c]
+        size = 8 * (stop - start)
+        v = CR[:, ds8(first + 8 * start, size), :].reshape(DEPTH * size, 256)
+        return reorder(v, order).reshape(DEPTH, size, 256)
+
+    load_cot.wait()
     xc = []
     for c in range(len(in_chunks)):
-        start, stop = in_chunks[c]
+        v = cot_rows(c, mate_base)
         for h in range(2):
-            copy = remote(
-                cot_h.at[0, :, ds8(mate_base + 8 * start, 8 * (stop - start)), lanes(h)],
-                C.at[pl.ds(own, DEPTH), h, c_rows(c), :],
-                xc_send.at[c, h], xc_recv.at[c, h], mate, r,
-            )
-            copy.start()
-            xc.append(copy)
-
-    table = [0.25 / jnp.full((1, 1, 8, 128), eps_s[j], F32) for j in range(16)]
+            SC[:, h, c_rows(c), :] = v[:, :, 128 * h : 128 * h + 128]
+        copy = remote(
+            SC.at[:, :, c_rows(c), :], C.at[pl.ds(own, DEPTH), :, c_rows(c), :], xc_send.at[c], xc_recv.at[c], mate, r
+        )
+        copy.start()
+        xc.append(copy)
+
+    table = [0.25 / jnp.full((1, 8, 128), eps_s[j], F32) for j in range(16)]
 
     def coefficient_of(index):
-        level = table
+        rows = index.shape[1] // 8
+        level = [jnp.concatenate([entry] * rows, 1) for entry in table]
         for bit in range(4):
             odd = ((index >> bit) & 1) != 0
             level = [jnp.where(odd, level[2 * j + 1], level[2 * j]) for j in range(len(level) // 2)]
         return level[0]
 
-    loads[0].wait()
-    loads[2].wait()
+    def material_rows(c, first):
+        start, stop = in_chunks[c]
+        size = 8 * (stop - start)
+        v = MT[:, ds8(first + 8 * start, size), :].reshape(DEPTH * size, 256).astype(F32).astype(jnp.bfloat16)
+        return jnp.dot(v, order, preferred_element_type=F32).reshape(DEPTH, size, 256)
+
+    load_material.wait()
     xk = []
     for c in range(len(in_chunks)):
-        start, stop = in_chunks[c]
-
-        def mates_rows(t, carry):
-            SK[:, :, ds8(PAD + 8 * t, 8), :] = coefficient_of(MT[:, :, ds8(mate_base + 8 * t, 8), :])
-            return carry
-
-        lax.fori_loop(start, stop, mates_rows, 0)
+        v = material_rows(c, mate_base)
+        v = jnp.where(core == 0, v[:, :, :128], v[:, :, 128:])
+        SK[:, c_rows(c), :] = coefficient_of(v.astype(jnp.int32))
         copy = remote(
-            SK.at[:, :, k_rows(c), :], K.at[pl.ds(own - 1, DEPTH), :, k_rows(c), :],
+            SK.at[:, k_rows(c), :], K.at[pl.ds(own - 1, DEPTH), core, k_rows(c), :],
             xk_send.at[c], xk_recv.at[c], mate, other_run,
         )
         copy.start()
         xk.append(copy)
-
-    def own_rows(t, carry):
-        K[pl.ds(own - 1, DEPTH), :, ds8(PAD + 8 * t, 8), :] = coefficient_of(MT[:, :, ds8(base + 8 * t, 8), :])
-        return carry
-
-    lax.fori_loop(0, tiles, own_rows, 0)
+    for c in range(len(in_chunks)):
+        v = cot_rows(c, base)
+        index = material_rows(c, base).astype(jnp.int32)
+        for h in range(2):
+            C[pl.ds(own, DEPTH), h, c_rows(c), :] = v[:, :, 128 * h : 128 * h + 128]
+            K[pl.ds(own - 1, DEPTH), h, c_rows(c), :] = coefficient_of(index[:, :, 128 * h : 128 * h + 128])
 
     remote(gath.at[mate], gath.at[mate], ag_send.at[0], ag_recv.at[0], mate, r).wait_recv()
     ag_z = []
@@ -234,55 +257,69 @@
         copy.start()
         ag_z.append(copy)
 
-    loads[1].wait()
-    loads[3].wait()
-
     def z_copy(c, kind, up):
+        way = 0 if up else 1
+        target = s + 2 if up else s - 2
         if kind == 0:
-            ref, rows, size = C, c_rows(c), STEPS
             src, dst = (FIRST + 2, 0) if up else (FIRST, FIRST + 2 * DEPTH)
+            src_ref = C.at[pl.ds(src, STEPS), :, c_rows(c), :]
+            dst_ref = C.at[pl.ds(dst, STEPS), :, c_rows(c), :]
         else:
-            ref, rows, size = K, k_rows(c), STEPS - 1
             src, dst = (FIRST + 2, 0) if up else (FIRST - 1, FIRST + 2 * DEPTH - 1)
-        way = 0 if up else 1
-        return remote(
-            ref.at[pl.ds(src, size), :, rows, :], ref.at[pl.ds(dst, size), :, rows, :],
-            z_send.at[way, kind, c], z_recv.at[way, kind, c], s + 2 if up else s - 2, r,
-        )
+            src_ref = K.at[pl.ds(src, STEPS - 1), core, k_rows(c), :]
+            dst_ref = K.at[pl.ds(dst, STEPS - 1), core, k_rows(c), :]
+        return remote(src_ref, dst_ref, z_send.at[way, kind, c], z_recv.at[way, kind, c], target, r)
+
+    def share(c, part, h):
+        first, size = ((mates - 1, DEPTH), (0, STEPS - 1), (FIRST + 2 * DEPTH - 1, STEPS - 1))[part]
+        ref = K.at[pl.ds(first, size), h, k_rows(c), :]
+        return remote(ref, ref, sib_send.at[part, c], sib_recv.at[part, c], s, other_core)
 
     def pass_on(c):
-        start, stop = in_chunks[c]
-        for h in range(2):
-            remote(
-                cot_h.at[0, :, ds8(mate_base + 8 * start, 8 * (stop - start)), lanes(h)],
-                C.at[pl.ds(mates, DEPTH), h, c_rows(c), :],
-                xc_send.at[c, h], xc_recv.at[c, h], mate, r,
-            ).wait_recv()
         remote(
-            SK.at[:, :, k_rows(c), :], K.at[pl.ds(mates - 1, DEPTH), :, k_rows(c), :],
+            SK.at[:, k_rows(c), :], K.at[pl.ds(mates - 1, DEPTH), core, k_rows(c), :],
             xk_send.at[c], xk_recv.at[c], mate, other_run,
         ).wait_recv()
+        remote(
+            SC.at[:, :, c_rows(c), :], C.at[pl.ds(mates, DEPTH), :, c_rows(c), :],
+            xc_send.at[c], xc_recv.at[c], mate, r,
+        ).wait_recv()
 
         @pl.when(not_last)
         def _():
-            for kind in range(2):
+            for kind in (1, 0):
                 z_copy(c, kind, True).start()
 
         @pl.when(not_first)
         def _():
-            for kind in range(2):
+            for kind in (1, 0):
                 z_copy(c, kind, False).start()
 
+        share(c, 0, core).start()
+
+    def pass_across(c):
+        @pl.when(not_first)
+        def _():
+            z_copy(c, 1, True).wait_recv()
+            share(c, 1, core).start()
+
+        @pl.when(not_last)
+        def _():
+            z_copy(c, 1, False).wait_recv()
+            share(c, 2, core).start()
+
     def halo_wait(c):
+        share(c, 0, 1 - core).wait_recv()
+
         @pl.when(not_first)
         def _():
-            for kind in range(2):
-                z_copy(c, kind, True).wait_recv()
+            z_copy(c, 0, True).wait_recv()
+            share(c, 1, 1 - core).wait_recv()
 
         @pl.when(not_last)
         def _():
-            for kind in range(2):
-                z_copy(c, kind, False).wait_recv()
+            z_copy(c, 0, False).wait_recv()
+            share(c, 2, 1 - core).wait_recv()
 
     pass_on(0)
 
@@ -320,7 +357,7 @@
     for d in range(1, grid_y):
         y_each(py, lambda full: y_copy(d, py, full).start())
     for c in range(1, len(in_chunks)):
-        if in_chunks[c][0] - 1 - LOOK < 0:
+        if PASS_AT[c] < 0:
             pass_on(c)
     for d in range(1, grid_y):
         source = lax.rem(py - d + grid_y, grid_y)
@@ -330,42 +367,30 @@
     is_last, is_first = lane == 127, lane == 0
 
     def up_z(v):
-        turned = pltpu.roll(v, 127, v.ndim - 1)
-        follow = jnp.concatenate([turned[1:2], jnp.zeros_like(turned[1:2])], 0)
-        return jnp.where(is_last if v.ndim == 4 else is_last[0], follow, turned)
+        turned = pltpu.roll(v[0:1], 127, v.ndim - 1)
+        turned = jnp.where(is_last if v.ndim == 4 else is_last[0], 0.0, turned)
+        return jnp.concatenate([v[1:2], turned], 0)
 
     def down_z(v):
-        turned = pltpu.roll(v, 1, v.ndim - 1)
-        before = jnp.concatenate([jnp.zeros_like(turned[0:1]), turned[0:1]], 0)
-        return jnp.where(is_first if v.ndim == 4 else is_first[0], before, turned)
-
-    for n in range(STEPS):
-
-        def port_rows(t, carry):
-            rows = ds8(PAD + 8 * t, 8)
-            slot = window + t
-            drive = (0.5 * forcing_of(n)) * gath[slot, pl.ds(0, 2)]
-            if n == 0:
-                W[0, :, rows, :] = drive
-                return carry
-            now = W[n - 1, :, rows, :]
-            after = W[n - 1, :, pl.ds(PAD + 8 * t + 1, 8), :]
-            before = W[n - 1, :, pl.ds(PAD + 8 * t - 1, 8), :]
-            laplacian = after + before + up_z(now) + down_z(now) - 4.0 * now
-            value = 2.0 * now + gath[slot, pl.ds(2, 2)] * laplacian + drive
-            if n > 1:
-                value = value - W[n - 2, :, rows, :]
-            W[n, :, rows, :] = value
-            return carry
-
-        lax.fori_loop(0, tiles, port_rows, 0)
+        turned = pltpu.roll(v[1:2], 1, v.ndim - 1)
+        turned = jnp.where(is_first if v.ndim == 4 else is_first[0], 0.0, turned)
+        return jnp.concatenate([turned, v[0:1]], 0)
 
     inside = not_first.astype(F32)
 
-    def source_of(n, rows):
-        ie = W[n - 1, :, rows, :]
-        ih = ie if n == 1 else ie - W[n - 2, :, rows, :]
-        return ie, ih
+    def source_of(n, t, rows, ahead_rows, behind_rows):
+        slot = window + t
+        drive = (0.5 * forcing_of(n - 1)) * gath[slot, pl.ds(0, 2)]
+        if n == 1:
+            W[0, :, rows, :] = drive
+            return drive, drive
+        now = W[n - 2, :, rows, :]
+        around = W[n - 2, :, ahead_rows, :] + W[n - 2, :, behind_rows, :] + up_z(now) + down_z(now)
+        value = 2.0 * now + gath[slot, pl.ds(2, 2)] * (around - 4.0 * now) + drive
+        if n > 2:
+            value = value - W[n - 3, :, rows, :]
+        W[n - 1, :, rows, :] = value
+        return value, value - now
 
     def add_driven(v, extra):
         return jnp.concatenate([v[:, 0:1] + extra[:, None], v[:, 1:2]], 1)
@@ -376,7 +401,7 @@
     def first_step(t):
         rows = ds8(PAD + 8 * t, 8)
         ahead_rows, behind_rows = pl.ds(PAD + 8 * t + 1, 8), pl.ds(PAD + 8 * t - 1, 8)
-        ie, ih = source_of(1, rows)
+        ie, ih = source_of(1, t, rows, ahead_rows, behind_rows)
         zero = jnp.zeros((2, 8, 128), F32)
         both = lambda d, e: jnp.stack([d, e], 1)
         follow = C[0, :, rows, :]
@@ -412,7 +437,7 @@
     def later_step(n, t):
         rows = ds8(PAD + 8 * t, 8)
         ahead_rows, behind_rows = pl.ds(PAD + 8 * t + 1, 8), pl.ds(PAD + 8 * t - 1, 8)
-        ie, ih = source_of(n, rows)
+        ie, ih = source_of(n, t, rows, ahead_rows, behind_rows)
         ey_n, ez_n = EY[n - 2, :, :, rows, :], EZ[n - 2, :, :, rows, :]
         gy_l = gz_l = None
         for i in range(n - 1, LAYERS - n):
@@ -465,13 +490,13 @@
         for k in range(2):
             rows = ds8(half * k + 8 * first, 8 * (stop - first))
             src = fin.at[:, rows, :]
-            dst = grad_h.at[:, rows, pl.ds(pl.multiple_of(128 * core, 128), 128)]
+            dst = grad_h.at[:, core, rows, :]
             copies.append(
                 (
                     pltpu.make_async_copy(src, dst, fin_copy.at[k, j]),
                     remote(src, dst, fin_send.at[k, j], fin_recv.at[k, j], s, other_core),
                     remote(
-                        src, grad_h.at[:, rows, pl.ds(pl.multiple_of(128 * (1 - core), 128), 128)],
+                        src, grad_h.at[:, 1 - core, rows, :],
                         fin_send.at[k, j], fin_recv.at[k, j], s, other_core,
                     ),
                 )
@@ -481,20 +506,17 @@
     def field_copies(j):
         first, stop = out_chunks[j]
         size = 8 * (stop - first)
-        copies = []
-        for h in range(2):
-            src_rows = ds8(PAD + 8 * (p + first), size)
-            dst = out_h.at[0, :, ds8(half * p + 8 * first, size), lanes(h)]
-            back = out_h.at[0, :, ds8(half * (1 - p) + 8 * first, size), lanes(h)]
-            src = EY.at[pl.ds(mates - 1, DEPTH), h, 0, src_rows, :]
-            copies.append(
-                (
-                    pltpu.make_async_copy(EY.at[pl.ds(own - 1, DEPTH), h, 0, src_rows, :], dst, fo_copy.at[h, j]),
-                    remote(src, dst, fo_send.at[h, j], fo_recv.at[h, j], mate, r),
-                    remote(src, back, fo_send.at[h, j], fo_recv.at[h, j], mate, r),
-                )
+        src_rows = ds8(PAD + 8 * (p + first), size)
+        dst = out_h.at[:, :, ds8(half * p + 8 * first, size), :]
+        back = out_h.at[:, :, ds8(half * (1 - p) + 8 * first, size), :]
+        src = EY.at[pl.ds(mates - 1, DEPTH), :, 0, src_rows, :]
+        return [
+            (
+                pltpu.make_async_copy(EY.at[pl.ds(own - 1, DEPTH), :, 0, src_rows, :], dst, fo_copy.at[j]),
+                remote(src, dst, fo_send.at[j], fo_recv.at[j], mate, r),
+                remote(src, back, fo_send.at[j], fo_recv.at[j], mate, r),
             )
-        return copies
+        ]
 
     def rows_done(j):
         near_copy(j).start()
@@ -535,8 +557,9 @@
     before, after, late = {}, {}, []
     for c in range(1, len(in_chunks)):
         at = in_chunks[c][0] - 1
-        if at - LOOK >= 0:
-            before.setdefault(at - LOOK, []).append(functools.partial(pass_on, c))
+        if PASS_AT[c] >= 0:
+            before.setdefault(PASS_AT[c], []).append(functools.partial(pass_on, c))
+        before.setdefault(max(0, at - 2), []).append(functools.partial(pass_across, c))
         before.setdefault(at, []).append(functools.partial(halo_wait, c))
     for j in range(len(out_chunks)):
         at = out_chunks[j][1] + STEPS - 1
@@ -555,6 +578,7 @@
                 for event in events:
                     event()
 
+    pass_across(0)
     halo_wait(0)
 
     def sweep(T, carry):
@@ -587,14 +611,17 @@
     for d in range(1, grid_y):
         y_each(py, lambda full: y_copy(d, py, full).wait_send())
     for c in range(len(in_chunks)):
+        share(c, 0, core).wait_send()
 
         @pl.when(not_last)
         def _():
+            share(c, 2, core).wait_send()
             for kind in range(2):
                 z_copy(c, kind, True).wait_send()
 
         @pl.when(not_first)
         def _():
+            share(c, 1, core).wait_send()
             for kind in range(2):
                 z_copy(c, kind, False).wait_send()
 
@@ -603,7 +630,7 @@
     tiles = slabs // 2 + 1
     height = 8 * tiles + 2 * PAD
     half, rows = 4 * slabs, 8 * slabs
-    chunks, outs = len(cuts(tiles, (3, 3, 4, 4, 3))), len(cuts(tiles - 1, (6, 5, 3, 2)))
+    chunks, outs = len(cuts(tiles, IN_SIZES)), len(cuts(tiles - 1, OUT_SIZES))
     vmem = lambda *shape: pltpu.VMEM(shape, F32)
     dma = lambda *shape: pltpu.SemaphoreType.DMA(shape)
     field = lambda layers: vmem(layers, 2, 2, height, 128)
@@ -614,7 +641,9 @@
         vmem(LAYERS, 2, height, 128),
         vmem(LAYERS - 2, 2, height, 128),
         vmem(DEPTH, 2, height, 128),
-        pltpu.VMEM((DEPTH, 2, rows, 128), jnp.int32),
+        vmem(DEPTH, height, 128),
+        pltpu.VMEM((DEPTH, rows, 256), jnp.int32),
+        vmem(DEPTH, rows, 256),
         field(LAYERS - 2), field(LAYERS - 2), field(LAYERS - 2),
         field(LAYERS - 1), field(LAYERS - 1), field(LAYERS - 1),
         vmem(2 * DEPTH, 2, height, 128),
@@ -622,17 +651,16 @@
         vmem(slabs, 4, 8, 128),
         vmem(2 * DEPTH, half, 128), vmem(2 * DEPTH, half, 128),
         vmem(DEPTH, half, 128), vmem(2, DEPTH, half, 128), vmem(DEPTH, rows, 128),
-        dma(4), dma(grid_z + grid_y - 1), dma(grid_z + grid_y - 1),
-        dma(chunks, 2), dma(chunks, 2), dma(chunks), dma(chunks), dma(2, 2, chunks), dma(2, 2, chunks),
+        dma(2), dma(grid_z + grid_y - 1), dma(grid_z + grid_y - 1),
+        dma(chunks), dma(chunks), dma(chunks), dma(chunks), dma(2, 2, chunks), dma(2, 2, chunks),
+        dma(3, chunks), dma(3, chunks),
         dma(outs), dma(outs), dma(3, outs), dma(3, outs),
-        dma(2, outs), dma(2, outs), dma(2, outs), dma(2, outs), dma(2, outs), dma(2, outs),
+        dma(2, outs), dma(2, outs), dma(2, outs), dma(outs), dma(outs), dma(outs),
     ]
-    return pl.pallas_call(
+    split = jax.ShapeDtypeStruct((DEPTH, 2, rows, 128), F32)
+    grad_p, field_p = pl.pallas_call(
         functools.partial(kernel, slabs, grid_y, grid_z),
-        out_shape=(
-            jax.ShapeDtypeStruct(material.shape, F32),
-            jax.ShapeDtypeStruct(cotangent.shape, F32),
-        ),
+        out_shape=(split, split),
         in_specs=[smem_spec, smem_spec, smem_spec, vmem_spec, vmem_spec, any_spec, any_spec],
         out_specs=(any_spec, any_spec),
         scratch_shapes=scratch,
@@ -641,6 +669,21 @@
         ),
         cost_estimate=pl.CostEstimate(flops=600_000_000, bytes_accessed=6_000_000, transcendentals=0),
     )(eps_table, surface_mask, excite_map, mode_profiles, port_eps, material, cotangent)
+    halves = pl.BlockSpec((1, 2, rows, 128), lambda x: (x, 0, 0, 0))
+    return pl.pallas_call(
+        restore,
+        grid=(DEPTH,),
+        out_shape=(
+            jax.ShapeDtypeStruct(material.shape, F32),
+            jax.ShapeDtypeStruct(cotangent.shape, F32),
+        ),
+        in_specs=[halves, halves],
+        out_specs=(
+            pl.BlockSpec((1, rows, 256), lambda x: (x, 0, 0)),
+            pl.BlockSpec((1, 1, rows, 256), lambda x: (0, x, 0, 0)),
+        ),
+        compiler_params=pltpu.CompilerParams(vmem_limit_bytes=60 * 1024 * 1024),
+    )(grad_p, field_p)
 
 
 def solution(mesh):

time: 115 us -> 89.2 us (0.78); the launches traced: 115 us -> 87.6 us
  Pallas kernels: 110 us -> 86.4 us
  local copies, waits for them, and re-layouts: 3.35 us -> 0 us
    pallas_call x1, Pallas kernels: 110 us -> 81.9 us  [local(): pl.pallas_call(functools.partial(kernel, slabs, grid_y, grid_z), out_shap...]
    pallas_call x0 -> x1, Pallas kernels: none -> 4.45 us  [local(): pl.pallas_call(restore, grid=(DEPTH,), out_shape=(jax.ShapeDtypeStruct(ma...]
    unnamed x4 -> x0, local copies, waits for them, and re-layouts: 3.35 us -> none
where the time goes in v2:
time: 89.2 us; the launch traced here: 87.6 us
  Pallas kernels  86.4 us (97%)
  between operations  1.28 us (1%)
    pallas_call x1, Pallas kernels, local(): pl.pallas_call(functools.partial(kernel, slabs, grid_y, grid_z), out_shap...  81.9 us
    pallas_call x1, Pallas kernels, local(): pl.pallas_call(restore, grid=(DEPTH,), out_shape=(jax.ShapeDtypeStruct(ma...  4.45 us

profile of v2, /device:TPU:1, one launch (start us, length us, event | category | flops | bytes accessed | tf_op | source)
XLA Modules:
  0.0 87.6 jit_solution(12496494085471244469)
XLA Ops:
  1.3 81.9 %shard_map.86 = (f32[4,2,256,128]{3,2,1,0:T(8,128)}, f32[4,2,256,128]{3,2,1,0:T(8,128)}) custom-call(f32[16]{0:T(128)} %eps_s.1, s32[4]{0:T(128)} %mask_s.1, s32[1]{0:T(128)S(6)} %copy.9.excite_s, f32[4,8,256]{2,1,0:T(8,128)} %profiles_v.1, f32[8,256]{1,0:T(8,128)} %port_v.1, s32[4,256,256]{2,1,0:T(8,128)} %material_h.1, f32[1,4,256,256]{3,2,1,0:T(8,128)} %cot_h.1), custom_call_target="tpu_custom_call" | custom-call | flops 600000000 | bytes 6000000 | tf_op jit(solution)/shard_map/pallas_call | solution.py:661
  83.2 4.5 %shard_map.87 = (f32[4,256,256]{2,1,0:T(8,128)}, f32[1,4,256,256]{3,2,1,0:T(8,128)}) custom-call(f32[4,2,256,128]{3,2,1,0:T(8,128)} %get-tuple-element.4.grad_p, f32[4,2,256,128]{3,2,1,0:T(8,128)} %get-tuple-element.5.field_p), custom_call_target="tpu_custom_call" | custom-call | tf_op jit(solution)/shard_map/pallas_call | solution.py:673

commit v3 on v2

--- a/solution.py
+++ b/solution.py
@@ -15,7 +15,7 @@
 PAD = 8
 FIRST = STEPS
 IN_SIZES = (2, 3, 4, 4, 4)
-OUT_SIZES = (4, 4, 4, 2, 2)
+OUT_SIZES = (2, 2, 3, 3, 3, 2, 1)
 PASS_AT = (-1, -1, 0, 2, 5)
 
 
@@ -45,9 +45,8 @@
     high = v.astype(jnp.bfloat16)
     rest = v - high.astype(F32)
     middle = rest.astype(jnp.bfloat16)
-    low = (rest - middle.astype(F32)).astype(jnp.bfloat16)
     dot = lambda part: jnp.dot(part, order, preferred_element_type=F32)
-    return (dot(high) + dot(middle)) + dot(low)
+    return dot(high) + dot(middle)
 
 
 def restore(grad_p, field_p, grad, field):
@@ -61,7 +60,7 @@
     eps_s, mask_s, excite_s, profiles_v, port_v, material_h, cot_h,
     grad_h, out_h,
     C, K, SC, SK, MT, CR, EX, EY, EZ, GX, GY, GZ, GR, W, gath, near, part, far, side, fin,
-    load_sem, ag_send, ag_recv, xc_send, xc_recv, xk_send, xk_recv, z_send, z_recv, sib_send, sib_recv,
+    load_sem, port_send, port_recv, xc_send, xc_recv, xk_send, xk_recv, z_send, z_recv, sib_send, sib_recv,
     near_send, near_recv, far_send, far_recv, fin_copy, fin_send, fin_recv, fo_copy, fo_send, fo_recv,
 ):
     half = 4 * slabs
@@ -112,6 +111,7 @@
     hello(mate, other_run)
     hello(s, other_core)
     hello(s, other_run)
+
     for peer in z_mates + y_mates:
         hello(peer, r)
 
@@ -130,8 +130,8 @@
     order = z_order(False)
     port_block = reorder(jnp.concatenate([picked, port], 0), order)
     for h in range(2):
-        gath[s, h] = port_block[0:8, 128 * h : 128 * h + 128]
-        gath[s, 2 + h] = port_block[8:16, 128 * h : 128 * h + 128]
+        gath[py, 2 * pz + p, h] = port_block[0:8, 128 * h : 128 * h + 128]
+        gath[py, 2 * pz + p, 2 + h] = port_block[8:16, 128 * h : 128 * h + 128]
 
     zero_row = jnp.zeros((8, 128), F32)
     bottom = jnp.zeros((2, 2, 8, 128), F32)
@@ -188,30 +188,59 @@
         for h in range(2):
             K[own - 1 + j, h, pl.ds(0, 8), :] = tile
 
-    pl.semaphore_wait(
-        barrier, 4 + (grid_z - 1) + (grid_y - 1) + not_first.astype(jnp.int32) + not_last.astype(jnp.int32)
-    )
-
-    ag_pair = remote(gath.at[s], gath.at[s], ag_send.at[0], ag_recv.at[0], mate, r)
-    ag_pair.start()
+    column = 2 * pz + p
+    band = grid_y // 2
+
+    def y_rows(d, y):
+        rows = gath.at[y, column]
+        return remote(rows, rows, port_send.at[d - 1], port_recv.at[d - 1], y_mates[d - 1], r)
+
+    def mate_rows(place):
+        rows = gath.at[:, place]
+        return remote(rows, rows, port_send.at[grid_y - 1], port_recv.at[grid_y - 1], mate, r)
+
+    def z_rows(d, z):
+        rows = gath.at[pl.ds(band * p, band), pl.ds(2 * z, 2)]
+        k = grid_y + d - 1
+        return remote(rows, rows, port_send.at[k], port_recv.at[k], z_mates[d - 1], r)
+
+    def edge_rows(d):
+        rows = gath.at[band - p, (2 * grid_z - 1) * p]
+        k = grid_y + grid_z + d - 2
+        return remote(rows, rows, port_send.at[k], port_recv.at[k], z_mates[d - 1], r)
+
+    def at_edge(z):
+        return z == (grid_z - 1) * p
+
+    def port_to_mate():
+        for d in range(1, grid_y):
+            y_rows(d, lax.rem(py - d + grid_y, grid_y)).wait_recv()
+        mate_rows(column).start()
+
+    def port_along_z():
+        mate_rows(2 * pz + 1 - p).wait_recv()
+        for d in range(1, grid_z):
+            z_rows(d, pz).start()
+
+        @pl.when(at_edge(pz))
+        def _():
+            for d in range(1, grid_z):
+                edge_rows(d).start()
+
+    def port_wait():
+        for d in range(1, grid_z):
+            source = lax.rem(pz - d + grid_z, grid_z)
+            z_rows(d, source).wait_recv()
+
+            @pl.when(at_edge(source))
+            def _():
+                edge_rows(d).wait_recv()
 
     def cot_rows(c, first):
         start, stop = in_chunks[c]
         size = 8 * (stop - start)
         v = CR[:, ds8(first + 8 * start, size), :].reshape(DEPTH * size, 256)
         return reorder(v, order).reshape(DEPTH, size, 256)
-
-    load_cot.wait()
-    xc = []
-    for c in range(len(in_chunks)):
-        v = cot_rows(c, mate_base)
-        for h in range(2):
-            SC[:, h, c_rows(c), :] = v[:, :, 128 * h : 128 * h + 128]
-        copy = remote(
-            SC.at[:, :, c_rows(c), :], C.at[pl.ds(own, DEPTH), :, c_rows(c), :], xc_send.at[c], xc_recv.at[c], mate, r
-        )
-        copy.start()
-        xc.append(copy)
 
     table = [0.25 / jnp.full((1, 8, 128), eps_s[j], F32) for j in range(16)]
 
@@ -229,46 +258,63 @@
         v = MT[:, ds8(first + 8 * start, size), :].reshape(DEPTH * size, 256).astype(F32).astype(jnp.bfloat16)
         return jnp.dot(v, order, preferred_element_type=F32).reshape(DEPTH, size, 256)
 
-    load_material.wait()
-    xk = []
-    for c in range(len(in_chunks)):
+    def fill_mates(c):
+        v = cot_rows(c, mate_base)
+        for h in range(2):
+            SC[:, h, c_rows(c), :] = v[:, :, 128 * h : 128 * h + 128]
         v = material_rows(c, mate_base)
         v = jnp.where(core == 0, v[:, :, :128], v[:, :, 128:])
         SK[:, c_rows(c), :] = coefficient_of(v.astype(jnp.int32))
-        copy = remote(
-            SK.at[:, k_rows(c), :], K.at[pl.ds(own - 1, DEPTH), core, k_rows(c), :],
-            xk_send.at[c], xk_recv.at[c], mate, other_run,
-        )
-        copy.start()
-        xk.append(copy)
-    for c in range(len(in_chunks)):
+
+    def fill_own(c):
         v = cot_rows(c, base)
         index = material_rows(c, base).astype(jnp.int32)
         for h in range(2):
             C[pl.ds(own, DEPTH), h, c_rows(c), :] = v[:, :, 128 * h : 128 * h + 128]
             K[pl.ds(own - 1, DEPTH), h, c_rows(c), :] = coefficient_of(index[:, :, 128 * h : 128 * h + 128])
 
-    remote(gath.at[mate], gath.at[mate], ag_send.at[0], ag_recv.at[0], mate, r).wait_recv()
-    ag_z = []
-    for d in range(1, grid_z):
-        copy = remote(
-            gath.at[pl.ds(2 * m, 2)], gath.at[pl.ds(2 * m, 2)], ag_send.at[d], ag_recv.at[d], z_mates[d - 1], r
-        )
-        copy.start()
-        ag_z.append(copy)
-
-    def z_copy(c, kind, up):
+    def x_copies(c):
+        return [
+            remote(
+                SC.at[:, :, c_rows(c), :], C.at[pl.ds(own, DEPTH), :, c_rows(c), :], xc_send.at[c], xc_recv.at[c], mate, r
+            ),
+            remote(
+                SK.at[:, k_rows(c), :], K.at[pl.ds(own - 1, DEPTH), core, k_rows(c), :],
+                xk_send.at[c], xk_recv.at[c], mate, other_run,
+            ),
+        ]
+
+    def z_copy(c, kind, up, part):
         way = 0 if up else 1
         target = s + 2 if up else s - 2
+        middle = FIRST + DEPTH
+        low, high = (FIRST + 2, FIRST + 2 * DEPTH) if up else (FIRST, FIRST + STEPS)
+        shift = -2 * DEPTH if up else 2 * DEPTH
+        if kind == 1:
+            low, high = (low + 1, high) if up else (low, high - 1)
+        first, stop = (low, middle) if part == 0 else (middle, high)
         if kind == 0:
-            src, dst = (FIRST + 2, 0) if up else (FIRST, FIRST + 2 * DEPTH)
-            src_ref = C.at[pl.ds(src, STEPS), :, c_rows(c), :]
-            dst_ref = C.at[pl.ds(dst, STEPS), :, c_rows(c), :]
+            src_ref = C.at[pl.ds(first, stop - first), :, c_rows(c), :]
+            dst_ref = C.at[pl.ds(first + shift, stop - first), :, c_rows(c), :]
         else:
-            src, dst = (FIRST + 2, 0) if up else (FIRST - 1, FIRST + 2 * DEPTH - 1)
-            src_ref = K.at[pl.ds(src, STEPS - 1), core, k_rows(c), :]
-            dst_ref = K.at[pl.ds(dst, STEPS - 1), core, k_rows(c), :]
-        return remote(src_ref, dst_ref, z_send.at[way, kind, c], z_recv.at[way, kind, c], target, r)
+            src_ref = K.at[pl.ds(first - 1, stop - first), core, k_rows(c), :]
+            dst_ref = K.at[pl.ds(first - 1 + shift, stop - first), core, k_rows(c), :]
+        sems = (way, 2 * kind + part, c)
+        return remote(src_ref, dst_ref, z_send.at[sems], z_recv.at[sems], target, r)
+
+    def z_start(c, owns):
+        for q in range(2):
+            part = q if owns else 1 - q
+
+            @pl.when((p == q) & not_last)
+            def _():
+                for kind in (1, 0):
+                    z_copy(c, kind, True, part).start()
+
+            @pl.when((p == q) & not_first)
+            def _():
+                for kind in (1, 0):
+                    z_copy(c, kind, False, part).start()
 
     def share(c, part, h):
         first, size = ((mates - 1, DEPTH), (0, STEPS - 1), (FIRST + 2 * DEPTH - 1, STEPS - 1))[part]
@@ -285,27 +331,22 @@
             xc_send.at[c], xc_recv.at[c], mate, r,
         ).wait_recv()
 
-        @pl.when(not_last)
-        def _():
-            for kind in (1, 0):
-                z_copy(c, kind, True).start()
-
-        @pl.when(not_first)
-        def _():
-            for kind in (1, 0):
-                z_copy(c, kind, False).start()
-
+        if c > 0:
+            z_start(c, True)
+        z_start(c, False)
         share(c, 0, core).start()
 
     def pass_across(c):
         @pl.when(not_first)
         def _():
-            z_copy(c, 1, True).wait_recv()
+            for part in range(2):
+                z_copy(c, 1, True, part).wait_recv()
             share(c, 1, core).start()
 
         @pl.when(not_last)
         def _():
-            z_copy(c, 1, False).wait_recv()
+            for part in range(2):
+                z_copy(c, 1, False, part).wait_recv()
             share(c, 2, core).start()
 
     def halo_wait(c):
@@ -313,55 +354,41 @@
 
         @pl.when(not_first)
         def _():
-            z_copy(c, 0, True).wait_recv()
+            for part in range(2):
+                z_copy(c, 0, True, part).wait_recv()
             share(c, 1, 1 - core).wait_recv()
 
         @pl.when(not_last)
         def _():
-            z_copy(c, 0, False).wait_recv()
+            for part in range(2):
+                z_copy(c, 0, False, part).wait_recv()
             share(c, 2, 1 - core).wait_recv()
 
-    pass_on(0)
-
-    for d in range(1, grid_z):
-        source = (py * grid_z + lax.rem(pz - d + grid_z, grid_z)) * 2
-        remote(
-            gath.at[pl.ds(source, 2)], gath.at[pl.ds(source, 2)], ag_send.at[d], ag_recv.at[d], z_mates[d - 1], r
-        ).wait_recv()
-
-    group = 2 * grid_z
-
-    def whole(y):
-        return jnp.where(p == 0, y < grid_y // 2, y >= grid_y // 2)
-
-    def single(y):
-        return y == grid_y // 2 - p
-
-    single_slot = slabs // 2 - p
-
-    def y_copy(d, y, full):
-        slots = pl.ds(group * y, group) if full else pl.ds(single_slot, 1)
-        return remote(
-            gath.at[slots], gath.at[slots], ag_send.at[grid_z + d - 1], ag_recv.at[grid_z + d - 1], y_mates[d - 1], r
-        )
-
-    def y_each(y, action):
-        @pl.when(whole(y))
-        def _():
-            action(True)
-
-        @pl.when(single(y))
-        def _():
-            action(False)
-
+    load_cot.wait()
+    load_material.wait()
+    fill_mates(0)
+    fill_own(0)
+    pl.semaphore_wait(
+        barrier, 4 + (grid_z - 1) + (grid_y - 1) + not_first.astype(jnp.int32) + not_last.astype(jnp.int32)
+    )
     for d in range(1, grid_y):
-        y_each(py, lambda full: y_copy(d, py, full).start())
+        y_rows(d, py).start()
+    for copy in x_copies(0):
+        copy.start()
+    z_start(0, True)
     for c in range(1, len(in_chunks)):
+        fill_mates(c)
+        for copy in x_copies(c):
+            copy.start()
+        if c == 1:
+            port_to_mate()
+            pass_on(0)
+        if c == min(2, len(in_chunks) - 1):
+            port_along_z()
+    for c in range(1, len(in_chunks)):
+        fill_own(c)
         if PASS_AT[c] < 0:
             pass_on(c)
-    for d in range(1, grid_y):
-        source = lax.rem(py - d + grid_y, grid_y)
-        y_each(source, lambda full: y_copy(d, source, full).wait_recv())
 
     lane = lax.broadcasted_iota(jnp.int32, (1, 1, 8, 128), 3)
     is_last, is_first = lane == 127, lane == 0
@@ -380,13 +407,14 @@
 
     def source_of(n, t, rows, ahead_rows, behind_rows):
         slot = window + t
-        drive = (0.5 * forcing_of(n - 1)) * gath[slot, pl.ds(0, 2)]
+        port_rows = gath.at[slot // (2 * grid_z), lax.rem(slot, 2 * grid_z)]
+        drive = (0.5 * forcing_of(n - 1)) * port_rows[pl.ds(0, 2)]
         if n == 1:
             W[0, :, rows, :] = drive
             return drive, drive
         now = W[n - 2, :, rows, :]
         around = W[n - 2, :, ahead_rows, :] + W[n - 2, :, behind_rows, :] + up_z(now) + down_z(now)
-        value = 2.0 * now + gath[slot, pl.ds(2, 2)] * (around - 4.0 * now) + drive
+        value = 2.0 * now + port_rows[pl.ds(2, 2)] * (around - 4.0 * now) + drive
         if n > 2:
             value = value - W[n - 3, :, rows, :]
         W[n - 1, :, rows, :] = value
@@ -520,9 +548,6 @@
 
     def rows_done(j):
         near_copy(j).start()
-        for here, there, _ in field_copies(j):
-            there.start()
-            here.start()
 
     def sum_cores(j):
         first, stop = out_chunks[j]
@@ -536,6 +561,9 @@
         lax.fori_loop(first, stop, one, 0)
         for copy in far_copies(j):
             copy.start()
+        for here, there, _ in field_copies(j):
+            there.start()
+            here.start()
 
     def sum_chips(j):
         first, stop = out_chunks[j]
@@ -563,7 +591,7 @@
         before.setdefault(at, []).append(functools.partial(halo_wait, c))
     for j in range(len(out_chunks)):
         at = out_chunks[j][1] + STEPS - 1
-        for event, delay in ((rows_done, 0), (sum_cores, 2), (sum_chips, 5)):
+        for event, delay in ((rows_done, 0), (sum_cores, 2), (sum_chips, 6)):
             if at + delay < sweeps:
                 after.setdefault(at + delay, []).append(functools.partial(event, j))
             else:
@@ -579,6 +607,7 @@
                     event()
 
     pass_across(0)
+    port_wait()
     halo_wait(0)
 
     def sweep(T, carry):
@@ -606,24 +635,35 @@
         near_copy(j).wait_send()
         for copy in far_copies(j):
             copy.wait_send()
-    for copy in xc + xk + ag_z + [ag_pair]:
-        copy.wait_send()
     for d in range(1, grid_y):
-        y_each(py, lambda full: y_copy(d, py, full).wait_send())
+        y_rows(d, py).wait_send()
+    mate_rows(column).wait_send()
+    for d in range(1, grid_z):
+        z_rows(d, pz).wait_send()
+
+    @pl.when(at_edge(pz))
+    def _():
+        for d in range(1, grid_z):
+            edge_rows(d).wait_send()
+
     for c in range(len(in_chunks)):
         share(c, 0, core).wait_send()
+        for copy in x_copies(c):
+            copy.wait_send()
 
         @pl.when(not_last)
         def _():
             share(c, 2, core).wait_send()
             for kind in range(2):
-                z_copy(c, kind, True).wait_send()
+                for part in range(2):
+                    z_copy(c, kind, True, part).wait_send()
 
         @pl.when(not_first)
         def _():
             share(c, 1, core).wait_send()
             for kind in range(2):
-                z_copy(c, kind, False).wait_send()
+                for part in range(2):
+                    z_copy(c, kind, False, part).wait_send()
 
 
 def local(slabs, grid_y, grid_z, material, eps_table, surface_mask, excite_map, mode_profiles, port_eps, cotangent):
@@ -648,11 +688,11 @@
         field(LAYERS - 1), field(LAYERS - 1), field(LAYERS - 1),
         vmem(2 * DEPTH, 2, height, 128),
         vmem(STEPS, 2, height, 128),
-        vmem(slabs, 4, 8, 128),
+        vmem(grid_y, 2 * grid_z, 4, 8, 128),
         vmem(2 * DEPTH, half, 128), vmem(2 * DEPTH, half, 128),
         vmem(DEPTH, half, 128), vmem(2, DEPTH, half, 128), vmem(DEPTH, rows, 128),
-        dma(2), dma(grid_z + grid_y - 1), dma(grid_z + grid_y - 1),
-        dma(chunks), dma(chunks), dma(chunks), dma(chunks), dma(2, 2, chunks), dma(2, 2, chunks),
+        dma(2), dma(grid_y + 2 * grid_z - 2), dma(grid_y + 2 * grid_z - 2),
+        dma(chunks), dma(chunks), dma(chunks), dma(chunks), dma(2, 4, chunks), dma(2, 4, chunks),
         dma(3, chunks), dma(3, chunks),
         dma(outs), dma(outs), dma(3, outs), dma(3, outs),
         dma(2, outs), dma(2, outs), dma(2, outs), dma(outs), dma(outs), dma(outs),

time: 89.2 us -> 87.7 us (0.983)
  Pallas kernels: 86.4 us -> 85.5 us
where the time goes in v3:
time: 87.7 us; the launch traced here: 86.8 us
  Pallas kernels  85.5 us (97%)
  between operations  1.28 us (1%)
    pallas_call x1, Pallas kernels, local(): pl.pallas_call(functools.partial(kernel, slabs, grid_y, grid_z), out_shap...  81.2 us
    pallas_call x1, Pallas kernels, local(): pl.pallas_call(restore, grid=(DEPTH,), out_shape=(jax.ShapeDtypeStruct(ma...  4.32 us

profile of v3, /device:TPU:1, one launch (start us, length us, event | category | flops | bytes accessed | tf_op | source)
XLA Modules:
  0.0 86.8 jit_solution(4765083173674290959)
XLA Ops:
  1.3 81.2 %shard_map.86 = (f32[4,2,256,128]{3,2,1,0:T(8,128)}, f32[4,2,256,128]{3,2,1,0:T(8,128)}) custom-call(f32[16]{0:T(128)} %eps_s.1, s32[4]{0:T(128)} %mask_s.1, s32[1]{0:T(128)S(6)} %copy.9.excite_s, f32[4,8,256]{2,1,0:T(8,128)} %profiles_v.1, f32[8,256]{1,0:T(8,128)} %port_v.1, s32[4,256,256]{2,1,0:T(8,128)} %material_h.1, f32[1,4,256,256]{3,2,1,0:T(8,128)} %cot_h.1), custom_call_target="tpu_custom_call" | custom-call | flops 600000000 | bytes 6000000 | tf_op jit(solution)/shard_map/pallas_call | solution.py:701
  82.5 4.3 %shard_map.87 = (f32[4,256,256]{2,1,0:T(8,128)}, f32[1,4,256,256]{3,2,1,0:T(8,128)}) custom-call(f32[4,2,256,128]{3,2,1,0:T(8,128)} %get-tuple-element.4.grad_p, f32[4,2,256,128]{3,2,1,0:T(8,128)} %get-tuple-element.5.field_p), custom_call_target="tpu_custom_call" | custom-call | tf_op jit(solution)/shard_map/pallas_call | solution.py:713

commit v4 on v3

--- a/solution.py
+++ b/solution.py
@@ -15,7 +15,7 @@
 PAD = 8
 FIRST = STEPS
 IN_SIZES = (2, 3, 4, 4, 4)
-OUT_SIZES = (2, 2, 3, 3, 3, 2, 1)
+OUT_SIZES = (1, 2, 2, 2, 3, 3, 2, 1)
 PASS_AT = (-1, -1, 0, 2, 5)
 
 
@@ -546,8 +546,15 @@
             )
         ]
 
+    def fields_start(j):
+        for here, there, _ in field_copies(j):
+            there.start()
+            here.start()
+
     def rows_done(j):
         near_copy(j).start()
+        if j < len(out_chunks) - 2:
+            fields_start(j)
 
     def sum_cores(j):
         first, stop = out_chunks[j]
@@ -561,9 +568,8 @@
         lax.fori_loop(first, stop, one, 0)
         for copy in far_copies(j):
             copy.start()
-        for here, there, _ in field_copies(j):
-            there.start()
-            here.start()
+        if j >= len(out_chunks) - 2:
+            fields_start(j)
 
     def sum_chips(j):
         first, stop = out_chunks[j]
@@ -591,7 +597,7 @@
         before.setdefault(at, []).append(functools.partial(halo_wait, c))
     for j in range(len(out_chunks)):
         at = out_chunks[j][1] + STEPS - 1
-        for event, delay in ((rows_done, 0), (sum_cores, 2), (sum_chips, 6)):
+        for event, delay in ((rows_done, 0), (sum_cores, 1), (sum_chips, 5)):
             if at + delay < sweeps:
                 after.setdefault(at + delay, []).append(functools.partial(event, j))
             else:

time: 87.7 us -> 86.8 us (0.990)
  no operation moved by 1% of the time
where the time goes in v4:
time: 86.8 us; the launch traced here: 86.1 us
  Pallas kernels  84.8 us (98%)
  between operations  1.28 us (1%)
    pallas_call x1, Pallas kernels, local(): pl.pallas_call(functools.partial(kernel, slabs, grid_y, grid_z), out_shap...  80.5 us
    pallas_call x1, Pallas kernels, local(): pl.pallas_call(restore, grid=(DEPTH,), out_shape=(jax.ShapeDtypeStruct(ma...  4.32 us

profile of v4, /device:TPU:1, one launch (start us, length us, event | category | flops | bytes accessed | tf_op | source)
XLA Modules:
  0.0 86.1 jit_solution(3955649165920892262)
XLA Ops:
  1.3 80.5 %shard_map.86 = (f32[4,2,256,128]{3,2,1,0:T(8,128)}, f32[4,2,256,128]{3,2,1,0:T(8,128)}) custom-call(f32[16]{0:T(128)} %eps_s.1, s32[4]{0:T(128)} %mask_s.1, s32[1]{0:T(128)S(6)} %copy.9.excite_s, f32[4,8,256]{2,1,0:T(8,128)} %profiles_v.1, f32[8,256]{1,0:T(8,128)} %port_v.1, s32[4,256,256]{2,1,0:T(8,128)} %material_h.1, f32[1,4,256,256]{3,2,1,0:T(8,128)} %cot_h.1), custom_call_target="tpu_custom_call" | custom-call | flops 600000000 | bytes 6000000 | tf_op jit(solution)/shard_map/pallas_call | solution.py:707
  81.8 4.3 %shard_map.87 = (f32[4,256,256]{2,1,0:T(8,128)}, f32[1,4,256,256]{3,2,1,0:T(8,128)}) custom-call(f32[4,2,256,128]{3,2,1,0:T(8,128)} %get-tuple-element.4.grad_p, f32[4,2,256,128]{3,2,1,0:T(8,128)} %get-tuple-element.5.field_p), custom_call_target="tpu_custom_call" | custom-call | tf_op jit(solution)/shard_map/pallas_call | solution.py:719

commit v5 on v4

--- a/solution.py
+++ b/solution.py
@@ -715,18 +715,18 @@
         ),
         cost_estimate=pl.CostEstimate(flops=600_000_000, bytes_accessed=6_000_000, transcendentals=0),
     )(eps_table, surface_mask, excite_map, mode_profiles, port_eps, material, cotangent)
-    halves = pl.BlockSpec((1, 2, rows, 128), lambda x: (x, 0, 0, 0))
+    halves = pl.BlockSpec((1, 2, half, 128), lambda x, y: (x, 0, y, 0))
     return pl.pallas_call(
         restore,
-        grid=(DEPTH,),
+        grid=(DEPTH, 2),
         out_shape=(
             jax.ShapeDtypeStruct(material.shape, F32),
             jax.ShapeDtypeStruct(cotangent.shape, F32),
         ),
         in_specs=[halves, halves],
         out_specs=(
-            pl.BlockSpec((1, rows, 256), lambda x: (x, 0, 0)),
-            pl.BlockSpec((1, 1, rows, 256), lambda x: (0, x, 0, 0)),
+            pl.BlockSpec((1, half, 256), lambda x, y: (x, y, 0)),
+            pl.BlockSpec((1, 1, half, 256), lambda x, y: (0, x, y, 0)),
         ),
         compiler_params=pltpu.CompilerParams(vmem_limit_bytes=60 * 1024 * 1024),
     )(grad_p, field_p)

time: 86.8 us -> 89.2 us (1.028)
  Pallas kernels: 84.8 us -> 87.1 us
    pallas_call x1, Pallas kernels: 4.32 us -> 6.58 us  [local(): pl.pallas_call(restore, grid=(DEPTH, 2), out_shape=(jax.ShapeDtypeStruct(...]
where the time goes in v5:
time: 89.2 us; the launch traced here: 88.4 us
  Pallas kernels  87.1 us (98%)
  between operations  1.28 us (1%)
    pallas_call x1, Pallas kernels, local(): pl.pallas_call(functools.partial(kernel, slabs, grid_y, grid_z), out_shap...  80.5 us
    pallas_call x1, Pallas kernels, local(): pl.pallas_call(restore, grid=(DEPTH, 2), out_shape=(jax.ShapeDtypeStruct(...  6.58 us

profile of v5, /device:TPU:1, one launch (start us, length us, event | category | flops | bytes accessed | tf_op | source)
XLA Modules:
  0.0 88.4 jit_solution(5404479680342760319)
XLA Ops:
  1.3 80.5 %shard_map.86 = (f32[4,2,256,128]{3,2,1,0:T(8,128)}, f32[4,2,256,128]{3,2,1,0:T(8,128)}) custom-call(f32[16]{0:T(128)} %eps_s.1, s32[4]{0:T(128)} %mask_s.1, s32[1]{0:T(128)S(6)} %copy.9.excite_s, f32[4,8,256]{2,1,0:T(8,128)} %profiles_v.1, f32[8,256]{1,0:T(8,128)} %port_v.1, s32[4,256,256]{2,1,0:T(8,128)} %material_h.1, f32[1,4,256,256]{3,2,1,0:T(8,128)} %cot_h.1), custom_call_target="tpu_custom_call" | custom-call | flops 600000000 | bytes 6000000 | tf_op jit(solution)/shard_map/pallas_call | solution.py:707
  81.8 6.6 %shard_map.87 = (f32[4,256,256]{2,1,0:T(8,128)}, f32[1,4,256,256]{3,2,1,0:T(8,128)}) custom-call(f32[4,2,256,128]{3,2,1,0:T(8,128)} %get-tuple-element.4.grad_p, f32[4,2,256,128]{3,2,1,0:T(8,128)} %get-tuple-element.5.field_p), custom_call_target="tpu_custom_call" | custom-call | tf_op jit(solution)/shard_map/pallas_call | solution.py:719
